TPU v7x, 256 devices: a whole 4x4x8 slice. The times are simulated.
256 devices in a mesh: shard: 128 (over y, x, z_lo, core), rep: 2 (over z_hi).
Axes of the slice: x: 4, y: 4, z: 8 (z_hi: 2, z_lo: 4; z = z_hi * 4 + z_lo), core: 2. Of those that a mesh axis runs over, the one named last changes fastest.
Arguments:
- dense_feats: bfloat16 [32768, 13], P(('shard', 'rep')), may hold values from -6 to 6
- lookup_ids: int32 [32768, 13, 4], P(('shard', 'rep')), may hold values from 0 to 8191, as said below
- bag_lengths: int32 [32768, 13], P(('shard', 'rep')), may hold values from 1 to 4
- bottom_w1: bfloat16 [13, 512], replicated, may hold values from -1.75 to 1.75
- bottom_w2: bfloat16 [512, 256], replicated, may hold values from -0.25 to 0.25
- bottom_w3: bfloat16 [256, 128], replicated, may hold values from -0.375 to 0.375
- tables: bfloat16 [13, 8192, 128], P(None, 'shard'), may hold values from -3 to 3
- accum: float32 [13, 8192], P(None, 'shard'), may hold values from 0.05 to 1
- cross_down: bfloat16 [1792, 512], replicated, may hold values from -0.125 to 0.125
- cross_up: bfloat16 [512, 1792], replicated, may hold values from -0.25 to 0.25
- cross_bias: float32 [1792], replicated, may hold values from -3 to 3
- cotangent: bfloat16 [32768, 1792], P(('shard', 'rep')), may hold values from -0.3984375 to 0.3984375
Outputs:
- crossed: bfloat16 [32768, 1792], P(('shard', 'rep'))
- new_tables: float32 [13, 8192, 128], P(None, 'shard')
- new_accum: float32 [13, 8192], P(None, 'shard')
Inputs may be any that keep to these rules, and one draw needn't show every extreme that they name: `lookup_ids`: row r of a table is held by index r // 64 of shard. Among the 6656 slots of one device (used or not), at most 78 name rows held by any one index of shard, and in every draw one index of shard gets exactly 78 from every device. Only the first bag_lengths[s, t] slots of bag (s, t) are used.
All inputs are finite; a program needn't handle non-finite values.
Results may differ from a plain program's by a relative error of at most 0.0065.
Values may be sent and summed in bfloat16 or wider, within the bound.
No kernel may reach another device: no remote copies, remote signals or barrier semaphores. Data moves between devices by JAX's collectives and lax.ppermute only.
A program may use at most 128 MiB of HBM per device.

v0:
```python
import jax
import jax.numpy as jnp
from jax import lax
from jax.sharding import PartitionSpec as P

step_size = 1.0
adagrad_eps = 1e-08
contract_first = (((0,), (0,)), ((), ()))
contract_last = (((1,), (1,)), ((), ()))


def from_everyone(x, axis):
    copies = jnp.broadcast_to(x, (lax.axis_size(axis), *x.shape))
    return lax.all_to_all(copies, axis, split_axis=0, concat_axis=0, tiled=True)


def of_everyone(x, axis):
    return from_everyone(x, axis).astype(jnp.float32).sum(axis=0)


def per_device(
    dense_feats,
    lookup_ids,
    bag_lengths,
    bottom_w1,
    bottom_w2,
    bottom_w3,
    tables,
    accum,
    cross_down,
    cross_up,
    cross_bias,
    cotangent,
):
    shards = lax.axis_size("shard")
    batch_rows, table_count, pool_slots = lookup_ids.shape
    rows_dev = tables.shape[1]
    emb_width = tables.shape[2]
    slot_count = batch_rows * table_count * pool_slots
    mean_load = slot_count // shards
    capacity = mean_load + mean_load // 2
    send_width = shards * capacity
    local_count = table_count * rows_dev
    owners = lookup_ids // rows_dev
    local_rows = (
        lookup_ids
        - owners * rows_dev
        + (jnp.arange(table_count, dtype=jnp.int32) * rows_dev)[None, :, None]
    )
    live_mask = jnp.arange(pool_slots, dtype=jnp.int32)[None, None, :] < bag_lengths[:, :, None]
    owner_flat = owners.reshape(-1)
    block_size = 128
    block_total = slot_count // block_size
    owner_marks = (owner_flat[:, None] == jnp.arange(shards, dtype=jnp.int32)[None, :]).astype(
        jnp.bfloat16
    )
    owner_marks = owner_marks.reshape(block_total, block_size, shards)
    earlier = (jnp.arange(block_size)[:, None] > jnp.arange(block_size)[None, :]).astype(
        jnp.bfloat16
    )
    within = jnp.einsum("ij,bjn->bin", earlier, owner_marks, preferred_element_type=jnp.float32)
    totals = jnp.sum(owner_marks, axis=1, dtype=jnp.float32)
    lower_blocks = (jnp.arange(block_total)[:, None] > jnp.arange(block_total)[None, :]).astype(
        jnp.float32
    )
    before = jnp.dot(lower_blocks, totals)
    positions = (
        jnp.sum((within + before[:, None, :]) * owner_marks, axis=2).reshape(-1).astype(jnp.int32)
    )
    slot_of = owner_flat * capacity + positions
    bag_count = batch_rows * table_count
    sample_block = min(64, batch_rows)
    block_rows = sample_block * table_count
    bag_blocks = bag_count // block_rows
    column_span = jnp.arange(send_width, dtype=jnp.int32)
    dest_blocks = slot_of.reshape(bag_blocks, block_rows, pool_slots)
    live_blocks = live_mask.reshape(bag_blocks, block_rows, pool_slots)

    def slot_marks(dest_part, live_part, slot):
        return (
            (dest_part[:, slot, None] == column_span[None, :]) & live_part[:, slot, None]
        ).astype(jnp.bfloat16)

    def bag_marks(dest_part, live_part):
        marks = slot_marks(dest_part, live_part, 0)
        for slot in range(1, pool_slots):
            marks = marks + slot_marks(dest_part, live_part, slot)
        return marks

    coded = jnp.where(live_mask, local_rows, -1).reshape(bag_blocks, block_rows, pool_slots) + 1
    digits = jnp.stack([coded % 128, coded // 128], axis=3).astype(jnp.float32).astype(jnp.bfloat16)

    def add_ids(carry, piece_list):
        dest_part, live_part, digit_part = piece_list
        for slot in range(pool_slots):
            carry = carry + lax.dot_general(
                slot_marks(dest_part, live_part, slot),
                digit_part[:, slot, :],
                contract_first,
                preferred_element_type=jnp.float32,
            )
        return (carry, None)

    digit_sum, _ = lax.scan(
        add_ids, jnp.zeros((send_width, 2), jnp.float32), (dest_blocks, live_blocks, digits)
    )
    send_ids = ((digit_sum[:, 0] + 128.0 * digit_sum[:, 1]).astype(jnp.int32) - 1).reshape(
        shards, capacity
    )
    table_rows_flat = tables.reshape(-1, emb_width)
    local_index = jnp.arange(local_count, dtype=jnp.int32)
    received = lax.all_to_all(send_ids, "shard", split_axis=0, concat_axis=0, tiled=True)
    row_flags = (received[..., None] == local_index).astype(jnp.bfloat16)
    picked = jnp.einsum(
        "ojk,kt->ojt", row_flags, table_rows_flat, preferred_element_type=jnp.float32
    ).astype(jnp.bfloat16)
    returned = lax.all_to_all(picked, "shard", split_axis=0, concat_axis=0, tiled=True)
    returned, owner_ids = (returned, received)
    returned_flat = returned.reshape(-1, emb_width)

    def pool_block(carry, piece_list):
        dest_part, live_part = piece_list
        return (
            carry,
            jnp.dot(
                bag_marks(dest_part, live_part), returned_flat, preferred_element_type=jnp.float32
            ),
        )

    _, pooled_blocks = lax.scan(pool_block, 0, (dest_blocks, live_blocks))
    pooled = pooled_blocks.reshape(batch_rows, table_count * emb_width)
    first_layer = jax.nn.relu(
        jnp.dot(dense_feats, bottom_w1, preferred_element_type=jnp.float32)
    ).astype(jnp.bfloat16)
    second_layer = jax.nn.relu(
        jnp.dot(first_layer, bottom_w2, preferred_element_type=jnp.float32)
    ).astype(jnp.bfloat16)
    third_layer = jax.nn.relu(
        jnp.dot(second_layer, bottom_w3, preferred_element_type=jnp.float32)
    ).astype(jnp.bfloat16)
    stacked = jnp.concatenate([third_layer, pooled.astype(jnp.bfloat16)], axis=1)
    low_rank = jnp.dot(stacked, cross_down, preferred_element_type=jnp.float32).astype(jnp.bfloat16)
    cross_hidden = jnp.dot(low_rank, cross_up, preferred_element_type=jnp.float32)
    widened = stacked.astype(jnp.float32)
    crossed = (widened * (cross_hidden + cross_bias) + widened).astype(jnp.bfloat16)
    cot_wide = cotangent.astype(jnp.float32)
    hidden_grad = (cot_wide * widened).astype(jnp.bfloat16)
    low_grad = lax.dot_general(
        hidden_grad, cross_up, contract_last, preferred_element_type=jnp.float32
    ).astype(jnp.bfloat16)
    back_term = lax.dot_general(
        low_grad, cross_down[emb_width:], contract_last, preferred_element_type=jnp.float32
    )
    pooled_grad = (
        cot_wide[:, emb_width:] * (cross_hidden[:, emb_width:] + cross_bias[emb_width:] + 1.0)
        + back_term
    ).astype(jnp.bfloat16)
    grad_blocks = pooled_grad.reshape(bag_blocks, block_rows, emb_width)

    def spread_block(carry, piece_list):
        dest_part, live_part, grad_part = piece_list
        return (
            carry
            + lax.dot_general(
                bag_marks(dest_part, live_part),
                grad_part,
                contract_first,
                preferred_element_type=jnp.float32,
            ),
            None,
        )

    spread, _ = lax.scan(
        spread_block,
        jnp.zeros((send_width, emb_width), jnp.float32),
        (dest_blocks, live_blocks, grad_blocks),
    )
    send_grads = spread.astype(jnp.bfloat16).reshape(shards, capacity, emb_width)
    received_rows = lax.all_to_all(send_grads, "shard", split_axis=0, concat_axis=0, tiled=True)
    target_flags = (owner_ids[..., None] == local_index).astype(jnp.bfloat16)
    group_grad = jnp.einsum(
        "jbp,jbm->pm", target_flags, received_rows, preferred_element_type=jnp.float32
    )
    accum_flat = accum.reshape(-1)
    row_grad = of_everyone(group_grad.astype(jnp.bfloat16), "rep").astype(jnp.float32)
    new_accum = accum_flat + jnp.mean(row_grad * row_grad, axis=1)
    new_tables = table_rows_flat.astype(jnp.float32) - step_size * row_grad / (
        jnp.sqrt(new_accum)[:, None] + adagrad_eps
    )
    return (
        crossed,
        new_tables.reshape(table_count, rows_dev, emb_width),
        new_accum.reshape(table_count, rows_dev),
    )


def solution(mesh):
    in_specs = (
        P(("shard", "rep"), None),
        P(("shard", "rep"), None, None),
        P(("shard", "rep"), None),
        P(),
        P(),
        P(),
        P(None, "shard", None),
        P(None, "shard"),
        P(),
        P(),
        P(),
        P(("shard", "rep"), None),
    )
    out_specs = (P(("shard", "rep"), None), P(None, "shard", None), P(None, "shard"))
    return jax.shard_map(
        per_device, mesh=mesh, in_specs=in_specs, out_specs=out_specs, check_vma=False
    )
```

profile of v0, /device:TPU:2, one launch (start us, length us, event | category | flops | bytes accessed | tf_op | source)
XLA Modules:
  0.0 469.1 jit_solution(12953326597942096360)
XLA Ops:
  7.7 86.4 %while.37 = (s32[]{:T(128)}, f32[9984,2]{0,1:T(2,128)S(1)}, s32[2,832,4]{1,2,0:T(4,128)S(1)}, pred[2,832,4]{1,2,0:T(4,128)(4,1)S(1)}, bf16[2,832,4,2]{1,3,2,0:T(2,128)(2,1)S(1)}, /*index=5*/s32[]{:T(128)}, s32[]{:T(128)}) while((s32[]{:T(128)}, f32[9984,2]{0,1:T(2,128)S(1)}, s32[2,832,4]{1,2,0:T(4,128)S(1)}, ...), condition=%wide.region_3.4_spmd.clone.clone, body=%wide.region_2.3_spmd.clone.clone.sunk | while | flops 199460352 | bytes 767075 | solution.py:104
  28.0 7.2 %fusion.165 = f32[9984,2]{0,1:T(2,128)S(1)} fusion(s32[832]{0:T(1024)S(1)} %get-tuple-element.462, pred[832]{0:T(1024)(128)(4,1)S(1)} %get-tuple-element.463, bf16[832,4,2]{0,2,1:T(2,128)(2,1)S(1)} %dynamic-slice_bitcast_fusion.18), kind=kOutput, calls=%fused_computation.43.clone.1 | convolution fusion | flops 49840128 | bytes 88576 | tf_op jit(solution)/shard_map/while/body/eval_jaxpr/dot_general | solution.py:96
  35.1 7.2 %fusion.166 = f32[9984,2]{0,1:T(2,128)S(1)} fusion(s32[832]{0:T(1024)S(1)} %get-tuple-element.464, pred[832]{0:T(1024)(128)(4,1)S(1)} %get-tuple-element.465, bf16[832,4,2]{0,2,1:T(2,128)(2,1)S(1)} %dynamic-slice_bitcast_fusion.18), kind=kOutput, calls=%fused_computation.44.clone.1 | convolution fusion | flops 49840128 | bytes 88576 | tf_op jit(solution)/shard_map/while/body/eval_jaxpr/dot_general | solution.py:96
  42.3 7.2 %fusion.167 = f32[9984,2]{0,1:T(2,128)S(1)} fusion(s32[832]{0:T(1024)S(1)} %get-tuple-element.466, pred[832]{0:T(1024)(128)(4,1)S(1)} %get-tuple-element.467, bf16[832,4,2]{0,2,1:T(2,128)(2,1)S(1)} %dynamic-slice_bitcast_fusion.18), kind=kOutput, calls=%fused_computation.45.clone.1 | convolution fusion | flops 49840128 | bytes 88576 | tf_op jit(solution)/shard_map/while/body/eval_jaxpr/dot_general | solution.py:96
  49.5 7.2 %fusion.168 = f32[9984,2]{0,1:T(2,128)S(1)} fusion(f32[9984,2]{0,1:T(2,128)S(1)} %fusion.165, f32[9984,2]{0,1:T(2,128)S(1)} %fusion.166, f32[9984,2]{0,1:T(2,128)S(1)} %fusion.167, s32[832]{0:T(1024)S(1)} %get-tuple-element.468, pred[832]{0:T(1024)(128)(4,1)S(1)} %get-tuple-element.469, f32[9984,2]{0,1:T(2,128)S(1)} %get-tuple-element.491, ...), kind=kOutput, calls=%fused_computation.58.clone.1 | convolution fusion | flops 49939968 | bytes 408065 | tf_op jit(solution)/shard_map/while/body/eval_jaxpr/dot_general | solution.py:96
  56.9 7.2 %fusion.165 = f32[9984,2]{0,1:T(2,128)S(1)} fusion(s32[832]{0:T(1024)S(1)} %get-tuple-element.462, pred[832]{0:T(1024)(128)(4,1)S(1)} %get-tuple-element.463, bf16[832,4,2]{0,2,1:T(2,128)(2,1)S(1)} %dynamic-slice_bitcast_fusion.18), kind=kOutput, calls=%fused_computation.43.clone.1 | convolution fusion | flops 49840128 | bytes 88576 | tf_op jit(solution)/shard_map/while/body/eval_jaxpr/dot_general | solution.py:96
  64.0 7.2 %fusion.166 = f32[9984,2]{0,1:T(2,128)S(1)} fusion(s32[832]{0:T(1024)S(1)} %get-tuple-element.464, pred[832]{0:T(1024)(128)(4,1)S(1)} %get-tuple-element.465, bf16[832,4,2]{0,2,1:T(2,128)(2,1)S(1)} %dynamic-slice_bitcast_fusion.18), kind=kOutput, calls=%fused_computation.44.clone.1 | convolution fusion | flops 49840128 | bytes 88576 | tf_op jit(solution)/shard_map/while/body/eval_jaxpr/dot_general | solution.py:96
  71.2 7.2 %fusion.167 = f32[9984,2]{0,1:T(2,128)S(1)} fusion(s32[832]{0:T(1024)S(1)} %get-tuple-element.466, pred[832]{0:T(1024)(128)(4,1)S(1)} %get-tuple-element.467, bf16[832,4,2]{0,2,1:T(2,128)(2,1)S(1)} %dynamic-slice_bitcast_fusion.18), kind=kOutput, calls=%fused_computation.45.clone.1 | convolution fusion | flops 49840128 | bytes 88576 | tf_op jit(solution)/shard_map/while/body/eval_jaxpr/dot_general | solution.py:96
  78.3 7.2 %fusion.168 = f32[9984,2]{0,1:T(2,128)S(1)} fusion(f32[9984,2]{0,1:T(2,128)S(1)} %fusion.165, f32[9984,2]{0,1:T(2,128)S(1)} %fusion.166, f32[9984,2]{0,1:T(2,128)S(1)} %fusion.167, s32[832]{0:T(1024)S(1)} %get-tuple-element.468, pred[832]{0:T(1024)(128)(4,1)S(1)} %get-tuple-element.469, f32[9984,2]{0,1:T(2,128)S(1)} %get-tuple-element.491, ...), kind=kOutput, calls=%fused_computation.58.clone.1 | convolution fusion | flops 49939968 | bytes 408065 | tf_op jit(solution)/shard_map/while/body/eval_jaxpr/dot_general | solution.py:96
  94.4 22.1 %all_to_all.21 = s32[128,1,78]{2,1,0:T(1,128)S(1)} all-to-all(s32[128,1,78]{2,1,0:T(1,128)S(1)} %bitcast.92), channel_id=1, replica_groups=mesh['shard'=128,'rep'=2] {'shard'}, dimensions={0} | all-to-all | bytes 79872 | tf_op jit(solution)/shard_map/all_to_all | solution.py:112
  116.5 9.8 %fusion.100 = bf16[128,78,128]{2,0,1:T(8,128)(2,1)S(1)} fusion(bf16[832,128,1]{1,0,2:T(8,128)(2,1)S(1)} %bitcast.94, s32[128,78]{0,1:T(8,128)S(1)} %copy.52), kind=kOutput, calls=%fused_computation.126 | convolution fusion | flops 2136096768 | bytes 2808832 | tf_op jit(solution)/shard_map/ojk,kt->ojt/dot_general | solution.py:114
  129.7 7.7 %all-to-all-start.1 = ((bf16[128,78,128]{2,1,0:T(8,128)(2,1)}), bf16[128,78,128]{2,1,0:T(8,128)(2,1)}, u32[]{:S(2)}, u32[]{:S(2)}) async-start(bf16[128,78,128]{2,1,0:T(8,128)(2,1)} %copy.53), calls=%async_computation.1 | async-start | bytes 5242880 | tf_op jit(solution)/shard_map/all_to_all | solution.py:117
  140.3 56.7 %all-to-all-done.1 = bf16[128,78,128]{2,1,0:T(8,128)(2,1)} async-done(((bf16[128,78,128]{2,1,0:T(8,128)(2,1)}), bf16[128,78,128]{2,1,0:T(8,128)(2,1)}, u32[]{:S(2)}, u32[]{:S(2)}) %all-to-all-start.1) | async-done | bytes 2555936 | tf_op jit(solution)/shard_map/all_to_all | solution.py:117
  197.0 4.9 %reshape.204 = bf16[9984,128]{1,0:T(8,128)(2,1)} reshape(bf16[128,78,128]{2,1,0:T(8,128)(2,1)} %all-to-all-done.1) | data formatting | bytes 5111808 | tf_op jit(solution)/shard_map/reshape | solution.py:119
  201.9 74.0 %while.36 = (s32[]{:T(128)}, bf16[2,832,128]{2,1,0:T(8,128)(2,1)S(1)}, s32[2,832,4]{1,2,0:T(4,128)S(1)}, pred[2,832,4]{1,2,0:T(4,128)(4,1)S(1)}, bf16[9984,128]{1,0:T(8,128)(2,1)}, /*index=5*/s32[]{:T(128)}) while((s32[]{:T(128)}, bf16[2,832,128]{2,1,0:T(8,128)(2,1)S(1)}, s32[2,832,4]{1,2,0:T(4,128)S(1)}, ...), condition=%wide.region_5.6_spmd.clone.clone, body=%wide.region_4.5_spmd.clone.clone.sunk | while | flops 2292645888 | bytes 3069009 | solution.py:130
  220.2 27.6 %fusion.160 = bf16[2,832,128]{2,1,0:T(8,128)(2,1)S(1)} fusion(bf16[2,832,128]{2,1,0:T(8,128)(2,1)S(1)} %get-tuple-element.511, s32[]{:T(128)} %get-tuple-element.510, bf16[9984,128]{1,0:T(8,128)(2,1)} %get-tuple-element.520, s32[832]{0:T(1024)S(1)} %get-tuple-element.449, s32[832]{0:T(1024)S(1)} %get-tuple-element.450, ...), kind=kOutput, calls=%fused_computation.24.clone.1 | convolution fusion | flops 2292645888 | bytes 3002372 | tf_op jit(solution)/shard_map/while/body/eval_jaxpr/dot_general | solution.py:125
  247.9 27.6 %fusion.160 = bf16[2,832,128]{2,1,0:T(8,128)(2,1)S(1)} fusion(bf16[2,832,128]{2,1,0:T(8,128)(2,1)S(1)} %get-tuple-element.511, s32[]{:T(128)} %get-tuple-element.510, bf16[9984,128]{1,0:T(8,128)(2,1)} %get-tuple-element.520, s32[832]{0:T(1024)S(1)} %get-tuple-element.449, s32[832]{0:T(1024)S(1)} %get-tuple-element.450, ...), kind=kOutput, calls=%fused_computation.24.clone.1 | convolution fusion | flops 2292645888 | bytes 3002372 | tf_op jit(solution)/shard_map/while/body/eval_jaxpr/dot_general | solution.py:125
  286.9 75.7 %while.38 = (s32[]{:T(128)}, f32[9984,128]{1,0:T(8,128)}, s32[2,832,4]{1,2,0:T(4,128)S(1)}, pred[2,832,4]{1,2,0:T(4,128)(4,1)S(1)}, bf16[2,832,128]{2,1,0:T(8,128)(2,1)S(1)}, /*index=5*/s32[]{:T(128)}, s32[]{:T(128)}) while((s32[]{:T(128)}, f32[9984,128]{1,0:T(8,128)}, s32[2,832,4]{1,2,0:T(4,128)S(1)}, ...), condition=%wide.region_7.8_spmd.clone.clone, body=%wide.region_6.7_spmd.clone.clone.sunk | while | flops 2295201792 | bytes 10523747 | solution.py:173
  294.9 29.3 %fusion.171 = f32[9984,128]{1,0:T(8,128)} fusion(s32[832]{0:T(1024)S(1)} %get-tuple-element.475, s32[832]{0:T(1024)S(1)} %get-tuple-element.476, s32[832]{0:T(1024)S(1)} %get-tuple-element.477, s32[832]{0:T(1024)S(1)} %get-tuple-element.478, pred[832]{0:T(1024)(128)(4,1)S(1)} %get-tuple-element.479, pred[832]{0:T(1024)(128)(4,1)S(1)} %get-tuple-element.480, ...), kind=kOutput, calls=%fused_computation.98.clone.1 | convolution fusion | flops 2295201792 | bytes 10457093 | tf_op jit(solution)/shard_map/while/body/eval_jaxpr/dot_general | solution.py:164
  324.3 31.8 %fusion.171 = f32[9984,128]{1,0:T(8,128)} fusion(s32[832]{0:T(1024)S(1)} %get-tuple-element.475, s32[832]{0:T(1024)S(1)} %get-tuple-element.476, s32[832]{0:T(1024)S(1)} %get-tuple-element.477, s32[832]{0:T(1024)S(1)} %get-tuple-element.478, pred[832]{0:T(1024)(128)(4,1)S(1)} %get-tuple-element.479, pred[832]{0:T(1024)(128)(4,1)S(1)} %get-tuple-element.480, ...), kind=kOutput, calls=%fused_computation.98.clone.1 | convolution fusion | flops 2295201792 | bytes 10457093 | tf_op jit(solution)/shard_map/while/body/eval_jaxpr/dot_general | solution.py:164
  366.3 4.9 %reshape.206 = bf16[128,78,128]{2,1,0:T(8,128)(2,1)} reshape(bf16[9984,128]{1,0:T(8,128)(2,1)} %convert_element_type.138) | data formatting | bytes 5111808 | tf_op jit(solution)/shard_map/reshape | solution.py:178
  371.2 69.9 %all_to_all.22 = bf16[128,78,128]{2,1,0:T(8,128)(2,1)S(1)} all-to-all(bf16[128,78,128]{2,1,0:T(8,128)(2,1)} %reshape.206), channel_id=1, replica_groups=mesh['shard'=128,'rep'=2] {'shard'}, dimensions={0} | all-to-all | bytes 5111808 | tf_op jit(solution)/shard_map/all_to_all | solution.py:179
  441.1 5.7 %fusion.106 = bf16[832,128]{1,0:T(8,128)(2,1)S(1)} fusion(bf16[128,78,128]{2,1,0:T(8,128)(2,1)S(1)} %all_to_all.22, s32[128,78]{0,1:T(8,128)S(1)} %copy-done.10), kind=kOutput, calls=%fused_computation.131 | convolution fusion | flops 2134925312 | bytes 2808832 | tf_op jit(solution)/shard_map/jbp,jbm->pm/dot_general | solution.py:181
  446.8 20.2 %all_to_all.23 = bf16[2,832,128]{2,1,0:T(8,128)(2,1)S(1)} all-to-all(bf16[2,832,128]{2,1,0:T(8,128)(2,1)S(1)} %broadcast_in_dim.16), channel_id=1, replica_groups=mesh['shard'=128,'rep'=2] {'rep'}, dimensions={0} | all-to-all | bytes 851968 | tf_op jit(solution)/shard_map/all_to_all | solution.py:14
  (107 shorter events, 30.8 us)
Async XLA Ops:
  0.6 277.6 %copy-start = (bf16[512,1792]{1,0:T(8,128)(2,1)S(1)}, bf16[512,1792]{1,0:T(8,128)(2,1)}, u32[]{:S(2)}) copy-start(bf16[512,1792]{1,0:T(8,128)(2,1)} %param.27) | copy-start | bytes 5505028
  7.7 108.9 %copy-start.6 = (bf16[13,64,128]{2,1,0:T(8,128)(2,1)S(1)}, bf16[13,64,128]{2,1,0:T(8,128)(2,1)}, u32[]{:S(2)}) copy-start(bf16[13,64,128]{2,1,0:T(8,128)(2,1)} %param.24) | copy-start | bytes 638980
  116.5 9.9 %copy-start.9 = (s32[128,78]{0,1:T(8,128)}, s32[128,78]{0,1:T(8,128)S(1)}, u32[]{:S(2)}) copy-start(s32[128,78]{0,1:T(8,128)S(1)} %copy.52) | copy-start | bytes 119812
  126.4 11.0 %copy-start.5 = (bf16[512,256]{1,0:T(8,128)(2,1)S(1)}, bf16[512,256]{1,0:T(8,128)(2,1)}, u32[]{:S(2)}) copy-start(bf16[512,256]{1,0:T(8,128)(2,1)} %param.22) | copy-start | bytes 786436
  126.4 11.0 %copy-start.13 = (bf16[13,512]{1,0:T(8,128)(2,1)S(1)}, bf16[13,512]{1,0:T(8,128)(2,1)}, u32[]{:S(2)}) copy-start(bf16[13,512]{1,0:T(8,128)(2,1)} %param.21) | copy-start | bytes 39940
  126.4 11.0 %copy-start.16 = (bf16[128,13]{0,1:T(8,128)(2,1)S(1)}, bf16[128,13]{0,1:T(8,128)(2,1)}, u32[]{:S(2)}) copy-start(bf16[128,13]{0,1:T(8,128)(2,1)} %param.18) | copy-start | bytes 9988
  126.4 11.3 %copy-start.8 = (bf16[256,128]{1,0:T(8,128)(2,1)S(1)}, bf16[256,128]{1,0:T(8,128)(2,1)}, u32[]{:S(2)}) copy-start(bf16[256,128]{1,0:T(8,128)(2,1)} %param.23) | copy-start | bytes 196612
  126.4 12.3 %copy-start.2 = (bf16[128,1792]{1,0:T(8,128)(2,1)S(1)}, bf16[128,1792]{1,0:T(8,128)(2,1)}, u32[]{:S(2)}) copy-start(bf16[128,1792]{1,0:T(8,128)(2,1)} %param.29) | copy-start | bytes 1376260
  126.5 13.2 %copy-start.11 = (f32[1792]{0:T(1024)S(1)}, f32[1792]{0:T(1024)}, u32[]{:S(2)}) copy-start(f32[1792]{0:T(1024)} %param.28) | copy-start | bytes 21508
  129.7 67.3 %all-to-all-start.1 = ((bf16[128,78,128]{2,1,0:T(8,128)(2,1)}), bf16[128,78,128]{2,1,0:T(8,128)(2,1)}, u32[]{:S(2)}, u32[]{:S(2)}) async-start(bf16[128,78,128]{2,1,0:T(8,128)(2,1)} %copy.53), calls=%async_computation.1 | async-start | bytes 5242880 | tf_op jit(solution)/shard_map/all_to_all | solution.py:117
  201.8 76.4 %copy-start.4 = (bf16[128,128]{1,0:T(8,128)(2,1)S(1)}, bf16[128,128]{1,0:T(8,128)(2,1)}, u32[]{:S(2)}) copy-start(bf16[128,128]{1,0:T(8,128)(2,1)} %copy.55) | copy-start | bytes 98308
  201.8 76.4 %copy-start.12 = (f32[1792]{0:T(1024)S(1)}, f32[1792]{0:T(1024)}, u32[]{:S(2)}) copy-start(f32[1792]{0:T(1024)} %param.28) | copy-start | bytes 21508
  275.9 0.8 copy-start.3
  276.6 5.0 %copy-start.1 = (f32[128,1792]{1,0:T(8,128)S(1)}, f32[128,1792]{1,0:T(8,128)}, u32[]{:S(2)}) copy-start(f32[128,1792]{1,0:T(8,128)} %convert_element_type.134) | copy-start | bytes 2752516
  276.6 5.0 %copy-start.14 = (f32[1664]{0:T(1024)S(1)}, f32[1664]{0:T(1024)}, u32[]{:S(2)}) copy-start(f32[1664]{0:T(1024)} %slice.106) | copy-start | bytes 19972
  366.3 74.8 %copy-start.10 = (s32[128,78]{0,1:T(8,128)S(1)}, s32[128,78]{0,1:T(8,128)}, u32[]{:S(2)}) copy-start(s32[128,78]{0,1:T(8,128)} %copy-done.9) | copy-start | bytes 119812
  441.1 26.3 %copy-start.15 = (f32[13,64]{1,0:T(8,128)S(1)}, f32[13,64]{1,0:T(8,128)}, u32[]{:S(2)}) copy-start(f32[13,64]{1,0:T(8,128)} %param.25) | copy-start | bytes 9988
  441.1 26.9 %copy-start.7 = (bf16[13,64,128]{2,1,0:T(8,128)(2,1)S(1)}, bf16[13,64,128]{2,1,0:T(8,128)(2,1)}, u32[]{:S(2)}) copy-start(bf16[13,64,128]{2,1,0:T(8,128)(2,1)} %param.24) | copy-start | bytes 638980
where the time goes:
time: 475 us; the launch traced here: 469 us
  matrix products  198 us (42%)
  blocking collectives  112 us (24%)
  loops' own time  61.7 us (13%)
  waiting for transfers between devices  56.7 us (12%)
  local copies, waits for them, and re-layouts  23 us (5%)
  other arithmetic  8.39 us (2%)
  starting transfers between devices  7.67 us (2%)
    all_to_all x1, blocking collectives, per_device(): lax.all_to_all(send_grads, 'shard', split_axis=0, concat_axis=0, tiled=True)  69.9 us
    dot_general x2, matrix products, spread_block(): lax.dot_general(bag_marks(dest_part, live_part), grad_part, contract_firs...  61.1 us
    dot_general x8, matrix products, add_ids(): lax.dot_general(slot_marks(dest_part, live_part, slot), digit_part[:, slo...  57.3 us
    all_to_all x1, waiting for transfers between devices, per_device(): lax.all_to_all(picked, 'shard', split_axis=0, concat_axis=0, tiled=True)  56.7 us
    dot_general x2, matrix products, pool_block(): jnp.dot(bag_marks(dest_part, live_part), returned_flat, preferred_element...  55.2 us
    another operation x1, loops' own time, per_device(): lax.scan(add_ids, jnp.zeros((send_width, 2), jnp.float32), (dest_blocks,...  28.7 us
    all_to_all x1, blocking collectives, per_device(): lax.all_to_all(send_ids, 'shard', split_axis=0, concat_axis=0, tiled=True)  22.1 us
    all_to_all x1, blocking collectives, from_everyone(): return lax.all_to_all(copies, axis, split_axis=0, concat_axis=0, tiled=True)  20.2 us
  transfers between devices with their start and end apart: 1, of which 1 were waited for; matrix products, arithmetic and copies ran while one was open for 1% of the time, Pallas kernels for 0%

commit v1 on v0

v1 whole, which is shorter than its diff:
```python
import jax
import jax.numpy as jnp
from jax import lax
from jax.experimental import pallas as pl
from jax.experimental.pallas import tpu as pltpu
from jax.sharding import PartitionSpec as P

f32, bf16, i32 = jnp.float32, jnp.bfloat16, jnp.int32
step_size = 1.0
adagrad_eps = 1e-08

CORES = 2
Z_LO = 4
COLUMN = CORES * Z_LO
GROUPS = 16
SHARDS = COLUMN * GROUPS
REPS = 2
Z = Z_LO * REPS
EMB = 128
LANES = 128
POOL = 4
ROWS_DEV = 64
PIECE = GROUPS * ROWS_DEV
HALF = Z_LO * PIECE
ROWS = CORES * HALF

across = [[g * COLUMN + k for g in range(GROUPS)] for k in range(COLUMN)]
swap_cores = [(s, s ^ 1) for s in range(SHARDS)]


def along_z(step):
    pairs = []
    for s in range(SHARDS):
        place, z_lo, core = s // COLUMN, (s // CORES) % Z_LO, s % CORES
        for r in range(REPS):
            z = (r * Z_LO + z_lo + step) % Z
            target = place * COLUMN + (z % Z_LO) * CORES + core
            pairs.append((s * REPS + r, target * REPS + z // Z_LO))
    return pairs


def send_z(x, step):
    return lax.ppermute(x, ("shard", "rep"), along_z(step))


def exchange(x):
    return lax.all_to_all(
        x, "shard", split_axis=0, concat_axis=0, axis_index_groups=across, tiled=True
    )


vmem = pl.BlockSpec(memory_space=pltpu.VMEM)
smem = pl.BlockSpec(memory_space=pltpu.SMEM)


def lookup(ids, parts, unroll=32):
    count = len(parts)
    places, samples = GROUPS, ids.shape[1]

    def body(ids_ref, *refs):
        part_refs, (out_ref, tab, acc) = refs[:count], refs[count:]
        at = 0
        for ref in part_refs:
            tab[at : at + ref.shape[0], :] = ref[...].astype(f32)
            at += ref.shape[0]
        tab[at : at + 8, :] = jnp.zeros((8, EMB), f32)

        def place(g, _):
            def some(i, _):
                for u in range(unroll):
                    s = i * unroll + u
                    r = [tab[pl.ds(ids_ref[g * POOL + j, s], 1), :] for j in range(POOL)]
                    acc[pl.ds(g * samples + s, 1), :] = (r[0] + r[1]) + (r[2] + r[3])
                return 0

            return lax.fori_loop(0, samples // unroll, some, 0)

        lax.fori_loop(0, places, place, 0)
        out_ref[...] = acc[...].astype(bf16)

    return pl.pallas_call(
        body,
        out_shape=jax.ShapeDtypeStruct((places * samples, EMB), bf16),
        in_specs=[smem] + [vmem] * count,
        out_specs=vmem,
        scratch_shapes=[
            pltpu.VMEM((ROWS + 8, EMB), f32),
            pltpu.VMEM((places * samples, EMB), f32),
        ],
        compiler_params=pltpu.CompilerParams(vmem_limit_bytes=40 << 20),
        name="lookup",
    )(ids, *parts)


def scatter(ids, grads, unroll=16):
    places, samples = GROUPS, ids.shape[1]

    def body(ids_ref, grads_ref, keep_ref, send_ref, a0, a1, a2, a3, wide):
        accs = (a0, a1, a2, a3)
        for a in accs:
            a[...] = jnp.zeros((ROWS + 8, EMB), f32)
        wide[...] = grads_ref[...].astype(f32)

        def place(g, _):
            def some(i, _):
                for u in range(unroll):
                    s = i * unroll + u
                    row = wide[pl.ds(g * samples + s, 1), :]
                    at = [ids_ref[g * POOL + j, s] for j in range(POOL)]
                    v = [accs[j][pl.ds(at[j], 1), :] for j in range(POOL)]
                    v = [x + row for x in v]
                    for j in range(POOL):
                        accs[j][pl.ds(at[j], 1), :] = v[j]
                return 0

            return lax.fori_loop(0, samples // unroll, some, 0)

        lax.fori_loop(0, places, place, 0)
        block = 512

        def total(at):
            sl = pl.ds(pl.multiple_of(at, block), block)
            return (a0[sl, :] + a1[sl, :]) + (a2[sl, :] + a3[sl, :])

        def finish(i, _):
            sl = pl.ds(pl.multiple_of(i * block, block), block)
            send_ref[sl, :] = total(HALF + i * block).astype(bf16)
            keep_ref[sl, :] = total(i * block)
            return 0

        lax.fori_loop(0, HALF // block, finish, 0)

    return pl.pallas_call(
        body,
        out_shape=[
            jax.ShapeDtypeStruct((HALF, EMB), f32),
            jax.ShapeDtypeStruct((HALF, EMB), bf16),
        ],
        in_specs=[smem, vmem],
        out_specs=[vmem, vmem],
        scratch_shapes=[pltpu.VMEM((ROWS + 8, EMB), f32)] * POOL
        + [pltpu.VMEM((places * samples, EMB), f32)],
        compiler_params=pltpu.CompilerParams(vmem_limit_bytes=50 << 20),
        name="scatter",
    )(ids, grads)


contract_last = (((1,), (1,)), ((), ()))


def cross(dense, w1, w2, w3, pooled, down, up, bias, cot):
    rows, width = cot.shape
    tables = width // EMB - 1

    def body(
        dense_ref, w1_ref, w2_ref, w3_ref, pooled_ref, down_ref, up_ref, bias_ref, cot_ref,
        crossed_ref, grad_ref, stacked,
    ):
        def dot(a, b):
            return jnp.dot(a, b, preferred_element_type=f32)

        first = jax.nn.relu(dot(dense_ref[...], w1_ref[...])).astype(bf16)
        second = jax.nn.relu(dot(first, w2_ref[...])).astype(bf16)
        stacked[:, :EMB] = jax.nn.relu(dot(second, w3_ref[...])).astype(bf16)
        for t in range(tables):
            stacked[:, (t + 1) * EMB : (t + 2) * EMB] = pooled_ref[t]
        low_rank = dot(stacked[...], down_ref[...]).astype(bf16)
        hidden_grad = (cot_ref[...].astype(f32) * stacked[...].astype(f32)).astype(bf16)
        low_grad = lax.dot_general(
            hidden_grad, up_ref[...], contract_last, preferred_element_type=f32
        ).astype(bf16)
        for t in range(tables + 1):
            cols = slice(t * EMB, (t + 1) * EMB)
            hidden = dot(low_rank, up_ref[:, cols]) + bias_ref[:, cols]
            wide = stacked[:, cols].astype(f32)
            crossed_ref[:, cols] = (wide * hidden + wide).astype(bf16)
            if t > 0:
                back = lax.dot_general(
                    low_grad, down_ref[cols, :], contract_last, preferred_element_type=f32
                )
                grad_ref[t - 1] = (cot_ref[:, cols].astype(f32) * (hidden + 1.0) + back).astype(
                    bf16
                )
        for t in range(tables, GROUPS):
            grad_ref[t] = jnp.zeros((rows, EMB), bf16)

    return pl.pallas_call(
        body,
        out_shape=[
            jax.ShapeDtypeStruct((rows, width), bf16),
            jax.ShapeDtypeStruct((GROUPS, rows, EMB), bf16),
        ],
        in_specs=[vmem] * 9,
        out_specs=[vmem, vmem],
        scratch_shapes=[pltpu.VMEM((rows, width), bf16)],
        compiler_params=pltpu.CompilerParams(vmem_limit_bytes=40 << 20),
        name="cross",
    )(dense, w1, w2, w3, pooled, down, up, bias.reshape(1, width), cot)


def per_device(
    dense_feats,
    lookup_ids,
    bag_lengths,
    bottom_w1,
    bottom_w2,
    bottom_w3,
    tables,
    accum,
    cross_down,
    cross_up,
    cross_bias,
    cotangent,
):
    samples, table_count, pool = lookup_ids.shape
    me = lax.axis_index("shard")
    my_core, my_z = me % CORES, (me // CORES) % Z_LO

    ids = jnp.transpose(lookup_ids, (1, 2, 0))
    used = jnp.arange(pool, dtype=i32)[None, :, None] < bag_lengths.T[:, None, :]
    owner, row = ids >> 6, ids & 63
    place, owner_z, owner_core = owner >> 3, (owner >> 1) & 3, owner & 1
    address = (
        (owner_core ^ my_core) * HALF + ((owner_z - my_z) & 3) * PIECE + place * ROWS_DEV + row
    )
    address = jnp.where(used, address, ROWS)
    digits = jnp.concatenate([address >> 7, address & 127], axis=1).astype(f32).astype(bf16)
    payload = jnp.concatenate([tables, digits], axis=1)
    payload = jnp.pad(payload, ((0, GROUPS - table_count), (0, 0), (0, 0)))
    got = exchange(payload)
    own = got[:, :ROWS_DEV].reshape(PIECE, EMB)
    high, low = got[:, ROWS_DEV : ROWS_DEV + pool], got[:, ROWS_DEV + pool :]
    at = (high.astype(f32) * 128.0 + low.astype(f32)).astype(i32).reshape(GROUPS * pool, samples)

    mid = PIECE // 2
    pieces = [
        own,
        send_z(own, -1),
        send_z(own[:mid], -2),
        send_z(own[mid:], 2),
        send_z(own, 1),
    ]
    others = [lax.ppermute(x, "shard", swap_cores) for x in pieces]
    pooled = exchange(lookup(at, pieces + others).reshape(GROUPS, samples, EMB))

    crossed, pooled_grad = cross(
        dense_feats, bottom_w1, bottom_w2, bottom_w3, pooled, cross_down, cross_up, cross_bias,
        cotangent,
    )
    grads = exchange(pooled_grad).reshape(GROUPS * samples, EMB)
    keep, send = scatter(at, grads)
    both = keep + lax.ppermute(send, "shard", swap_cores).astype(f32)
    part = [both[d * PIECE : (d + 1) * PIECE] for d in range(Z_LO)]

    up, dn = part[0], part[1]
    for d in (3, 2, 1):
        up = send_z(up.astype(bf16), 1).astype(f32) + part[d]
    up = send_z(up.astype(bf16), 1).astype(f32)
    for d in (2, 3):
        dn = send_z(dn.astype(bf16), -1).astype(f32) + part[d]
    dn = send_z(dn.astype(bf16), -1).astype(f32)
    summed = (part[0] + up + dn).astype(bf16).reshape(GROUPS, ROWS_DEV, EMB)
    row_grad = exchange(summed)[:table_count].astype(f32)
    new_accum = accum + jnp.mean(row_grad * row_grad, axis=2)
    new_tables = tables.astype(f32) - step_size * row_grad / (
        jnp.sqrt(new_accum)[:, :, None] + adagrad_eps
    )
    return crossed, new_tables, new_accum


def solution(mesh):
    in_specs = (
        P(("shard", "rep"), None),
        P(("shard", "rep"), None, None),
        P(("shard", "rep"), None),
        P(),
        P(),
        P(),
        P(None, "shard", None),
        P(None, "shard"),
        P(),
        P(),
        P(),
        P(("shard", "rep"), None),
    )
    out_specs = (P(("shard", "rep"), None), P(None, "shard", None), P(None, "shard"))
    return jax.shard_map(
        per_device, mesh=mesh, in_specs=in_specs, out_specs=out_specs, check_vma=False
    )
```

time: 475 us -> 157 us (0.33)
  matrix products: 198 us -> 0 us
  blocking collectives: 112 us -> 41.5 us
  loops' own time: 61.7 us -> 0 us
  Pallas kernels: 0 us -> 35.4 us
  local copies, waits for them, and re-layouts: 23 us -> 1.8 us
  starting transfers between devices: 7.67 us -> 26.1 us
  waiting for transfers between devices: 56.7 us -> 44.9 us
    dot_general x20 -> x0, matrix products: 198 us -> none  [the longest x2 61.1 us: spread_block(): lax.dot_general(bag_marks(dest_part, live_part), grad_part, contract_firs...]
    all_to_all x3, blocking collectives: 112 us -> 41.5 us  [exchange(): lax.all_to_all(x, 'shard', split_axis=0, concat_axis=0, axis_index_groups...]
    another operation x3 -> x0, loops' own time: 61.7 us -> none  [the longest x1 28.7 us: per_device(): lax.scan(add_ids, jnp.zeros((send_width, 2), jnp.float32), (dest_blocks,...]
    all_to_all x1, waiting for transfers between devices: 56.7 us -> 10.7 us  [exchange(): lax.all_to_all(x, 'shard', split_axis=0, concat_axis=0, axis_index_groups...]
    pallas_call x0 -> x3, Pallas kernels: none -> 35.4 us  [the longest x1 17.1 us: scatter(): pl.pallas_call(body, out_shape=[jax.ShapeDtypeStruct((HALF, EMB), f32), j...]
    ppermute x0 -> x17, waiting for transfers between devices: none -> 34.2 us  [the longest x11 30.3 us: send_z(): return lax.ppermute(x, ('shard', 'rep'), along_z(step))]
    ppermute x0 -> x17, starting transfers between devices: none -> 21.4 us  [the longest x11 21.2 us: send_z(): return lax.ppermute(x, ('shard', 'rep'), along_z(step))]
    reshape x3 -> x1, local copies, waits for them, and re-layouts: 11.3 us -> 0.01 us  [cross(): bias.reshape(1, width)]
  transfers between devices with their start and end apart: 1 -> 18, of which waited for: 1 -> 15; matrix products, arithmetic and copies ran while one was open for 1% -> 0% of each run, Pallas kernels for 0% -> 0%
where the time goes in v1:
time: 157 us; the launch traced here: 155 us
  waiting for transfers between devices  44.9 us (29%)
  blocking collectives  41.5 us (26%)
  Pallas kernels  35.4 us (23%)
  starting transfers between devices  26.1 us (17%)
  other arithmetic  4.13 us (3%)
  local copies, waits for them, and re-layouts  1.8 us (1%)
    all_to_all x3, blocking collectives, exchange(): lax.all_to_all(x, 'shard', split_axis=0, concat_axis=0, axis_index_groups...  41.5 us
    ppermute x11, waiting for transfers between devices, send_z(): return lax.ppermute(x, ('shard', 'rep'), along_z(step))  30.3 us
    ppermute x11, starting transfers between devices, send_z(): return lax.ppermute(x, ('shard', 'rep'), along_z(step))  21.2 us
    pallas_call x1, Pallas kernels, scatter(): pl.pallas_call(body, out_shape=[jax.ShapeDtypeStruct((HALF, EMB), f32), j...  17.1 us
    pallas_call x1, Pallas kernels, lookup(): pl.pallas_call(body, out_shape=jax.ShapeDtypeStruct((places * samples, EM...  15.2 us
    all_to_all x1, waiting for transfers between devices, exchange(): lax.all_to_all(x, 'shard', split_axis=0, concat_axis=0, axis_index_groups...  10.7 us
    all_to_all x1, starting transfers between devices, exchange(): lax.all_to_all(x, 'shard', split_axis=0, concat_axis=0, axis_index_groups...  4.79 us
  transfers between devices with their start and end apart: 18, of which 15 were waited for; matrix products, arithmetic and copies ran while one was open for 0% of the time, Pallas kernels for 0%

profile of v1, /device:TPU:2, one launch (start us, length us, event | category | flops | bytes accessed | tf_op | source)
XLA Modules:
  0.0 154.8 jit_solution(17582401628187900885)
XLA Ops:
  2.5 14.9 %all_to_all.20 = bf16[16,72,128]{2,1,0:T(8,128)(2,1)S(1)} all-to-all(bf16[16,72,128]{2,1,0:T(8,128)(2,1)S(1)} %fusion.4), channel_id=1, replica_groups={{0,16,32,48,64,80,96,112,128,144,160,176,192,208,224,240},{2,18,34,50,6..., dimensions={0} | all-to-all | bytes 589824 | tf_op jit(solution)/shard_map/all_to_all | solution.py:47
  17.5 2.0 %collective-permute-start.3 = (bf16[1024,128]{1,0:T(8,128)(2,1)S(1)}, bf16[1024,128]{1,0:T(8,128)(2,1)S(1)}, u32[]{:S(2)}, u32[]{:S(2)}) collective-permute-start(bf16[1024,128]{1,0:T(8,128)(2,1)S(1)} %bitcast.12), channel_id=1, source_target_pairs={{0,4},{1,5},{2,6},{3,7},{4,8},{5,9},{6,10},{7,11},{8,12},{9,13},{1... | collective-permute-start | bytes 786440 | tf_op jit(solution)/shard_map/ppermute | solution.py:43
  19.5 4.0 %collective-permute-start = (bf16[1024,128]{1,0:T(8,128)(2,1)S(1)}, bf16[1024,128]{1,0:T(8,128)(2,1)S(1)}, u32[]{:S(2)}, u32[]{:S(2)}) collective-permute-start(bf16[1024,128]{1,0:T(8,128)(2,1)S(1)} %bitcast.13), channel_id=1, source_target_pairs={{0,13},{1,12},{2,15},{3,14},{4,0},{5,1},{6,2},{7,3},{8,4},{9,5},{1... | collective-permute-start | bytes 786440 | tf_op jit(solution)/shard_map/ppermute | solution.py:43
  23.6 2.5 %collective-permute-start.1 = (bf16[512,128]{1,0:T(8,128)(2,1)S(1)}, bf16[512,128]{1,0:T(8,128)(2,1)S(1)}, u32[]{:S(2)}, u32[]{:S(2)}) collective-permute-start(bf16[512,128]{1,0:T(8,128)(2,1)S(1)} %bitcast.20), channel_id=1, source_target_pairs={{0,9},{1,8},{2,11},{3,10},{4,13},{5,12},{6,15},{7,14},{8,0},{9,1},... | collective-permute-start | bytes 393224 | tf_op jit(solution)/shard_map/ppermute | solution.py:43
  26.6 2.6 %collective-permute-done.3.refs_4_ = bf16[1024,128]{1,0:T(8,128)(2,1)S(1)} collective-permute-done((bf16[1024,128]{1,0:T(8,128)(2,1)S(1)}, bf16[1024,128]{1,0:T(8,128)(2,1)S(1)}, u32[]{:S(2)}, u32[]{:S(2)}) %collective-permute-start.3) | collective-permute-done | bytes 262176 | tf_op jit(solution)/shard_map/ppermute | solution.py:43
  29.1 3.0 %collective-permute-done.refs_1_ = bf16[1024,128]{1,0:T(8,128)(2,1)S(1)} collective-permute-done((bf16[1024,128]{1,0:T(8,128)(2,1)S(1)}, bf16[1024,128]{1,0:T(8,128)(2,1)S(1)}, u32[]{:S(2)}, u32[]{:S(2)}) %collective-permute-start) | collective-permute-done | bytes 262176 | tf_op jit(solution)/shard_map/ppermute | solution.py:43
  35.6 15.2 %lookup.1 = bf16[2048,128]{1,0:T(8,128)(2,1)} custom-call(s32[64,128]{1,0:T(8,128)S(1)} %bitcast.16, bf16[1024,128]{1,0:T(8,128)(2,1)S(1)} %bitcast.15, bf16[1024,128]{1,0:T(8,128)(2,1)S(1)} %collective-permute-done.refs_1_, bf16[512,128]{1,0:T(8,128)(2,1)S(1)} %collective-permute-done.1.refs_2_, bf16[512,128]{1,0:T(8,128)(2,1)S(1)} %collective-permute-done.2.refs_3_, ...), custom_call_target="tpu_custom_call" | custom-call | tf_op jit(solution)/shard_map/lookup/pallas_call | solution.py:81
  50.8 4.8 %all-to-all-start.1 = ((bf16[16,128,128]{2,1,0:T(8,128)(2,1)}), bf16[16,128,128]{2,1,0:T(8,128)(2,1)S(1)}, u32[]{:S(2)}, u32[]{:S(2)}) async-start(bf16[16,128,128]{2,1,0:T(8,128)(2,1)} %bitcast.6), calls=%async_computation.1 | async-start | bytes 1048576 | tf_op jit(solution)/shard_map/all_to_all | solution.py:47
  55.7 10.7 %all-to-all-done.1.pooled_ref = bf16[16,128,128]{2,1,0:T(8,128)(2,1)S(1)} async-done(((bf16[16,128,128]{2,1,0:T(8,128)(2,1)}), bf16[16,128,128]{2,1,0:T(8,128)(2,1)S(1)}, u32[]{:S(2)}, u32[]{:S(2)}) %all-to-all-start.1) | async-done | bytes 524320 | tf_op jit(solution)/shard_map/all_to_all | solution.py:47
  66.4 1.5 copy-done.1
  67.9 3.1 %cross.1 = (bf16[128,1792]{1,0:T(8,128)(2,1)}, bf16[16,128,128]{2,1,0:T(8,128)(2,1)S(1)}) custom-call(bf16[128,13]{1,0:T(8,128)(2,1)S(1)} %copy.15.dense_ref, bf16[13,512]{1,0:T(8,128)(2,1)S(1)} %copy-done.5, bf16[512,256]{1,0:T(8,128)(2,1)S(1)} %copy-done.3, bf16[256,128]{1,0:T(8,128)(2,1)S(1)} %copy-done.4, ...), custom_call_target="tpu_custom_call" | custom-call | tf_op jit(solution)/shard_map/cross/pallas_call | solution.py:187
  71.0 14.0 %all_to_all.21 = bf16[16,128,128]{2,1,0:T(8,128)(2,1)S(1)} all-to-all(bf16[16,128,128]{2,1,0:T(8,128)(2,1)S(1)} %get-tuple-element.8), channel_id=1, replica_groups={{0,16,32,48,64,80,96,112,128,144,160,176,192,208,224,240},{2,18,34,50,6..., dimensions={0} | all-to-all | bytes 1048576 | tf_op jit(solution)/shard_map/all_to_all | solution.py:47
  85.1 17.1 %scatter.1 = (f32[4096,128]{1,0:T(8,128)S(1)}, bf16[4096,128]{1,0:T(8,128)(2,1)S(1)}) custom-call(s32[64,128]{1,0:T(8,128)S(1)} %bitcast.17, bf16[2048,128]{1,0:T(8,128)(2,1)S(1)} %bitcast.11), custom_call_target="tpu_custom_call" | custom-call | tf_op jit(solution)/shard_map/scatter/pallas_call | solution.py:133
  102.3 2.6 %collective-permute-done.9 = bf16[4096,128]{1,0:T(8,128)(2,1)S(1)} collective-permute-done((bf16[4096,128]{1,0:T(8,128)(2,1)S(1)}, bf16[4096,128]{1,0:T(8,128)(2,1)S(1)}, u32[]{:S(2)}, u32[]{:S(2)}) %collective-permute-start.9) | collective-permute-done | bytes 1048608 | tf_op jit(solution)/shard_map/ppermute | solution.py:252
  105.2 2.1 %collective-permute-start.10 = (bf16[1024,128]{1,0:T(8,128)(2,1)S(1)}, bf16[1024,128]{1,0:T(8,128)(2,1)S(1)}, u32[]{:S(2)}, u32[]{:S(2)}) collective-permute-start(bf16[1024,128]{1,0:T(8,128)(2,1)S(1)} %get-tuple-element.19), channel_id=1, source_target_pairs={{0,4},{1,5},{2,6},{3,7},{4,8},{5,9},{6,10},{7,11},{8,12},{9,13},{1... | collective-permute-start | bytes 786440 | tf_op jit(solution)/shard_map/ppermute | solution.py:43
  108.7 6.3 %collective-permute-done.10 = bf16[1024,128]{1,0:T(8,128)(2,1)S(1)} collective-permute-done((bf16[1024,128]{1,0:T(8,128)(2,1)S(1)}, bf16[1024,128]{1,0:T(8,128)(2,1)S(1)}, u32[]{:S(2)}, u32[]{:S(2)}) %collective-permute-start.10) | collective-permute-done | bytes 262176 | tf_op jit(solution)/shard_map/ppermute | solution.py:43
  115.1 2.1 %collective-permute-start.11 = (bf16[1024,128]{1,0:T(8,128)(2,1)S(1)}, bf16[1024,128]{1,0:T(8,128)(2,1)S(1)}, u32[]{:S(2)}, u32[]{:S(2)}) collective-permute-start(bf16[1024,128]{1,0:T(8,128)(2,1)S(1)} %add_convert_fusion.5), channel_id=1, source_target_pairs={{0,4},{1,5},{2,6},{3,7},{4,8},{5,9},{6,10},{7,11},{8,12},{9,13},{1... | collective-permute-start | bytes 786440 | tf_op jit(solution)/shard_map/ppermute | solution.py:43
  117.5 6.4 %collective-permute-done.11 = bf16[1024,128]{1,0:T(8,128)(2,1)S(1)} collective-permute-done((bf16[1024,128]{1,0:T(8,128)(2,1)S(1)}, bf16[1024,128]{1,0:T(8,128)(2,1)S(1)}, u32[]{:S(2)}, u32[]{:S(2)}) %collective-permute-start.11) | collective-permute-done | bytes 262176 | tf_op jit(solution)/shard_map/ppermute | solution.py:43
  124.9 2.4 %collective-permute-start.15 = (bf16[1024,128]{1,0:T(8,128)(2,1)S(1)}, bf16[1024,128]{1,0:T(8,128)(2,1)S(1)}, u32[]{:S(2)}, u32[]{:S(2)}) collective-permute-start(bf16[1024,128]{1,0:T(8,128)(2,1)S(1)} %get-tuple-element.18), channel_id=1, source_target_pairs={{0,13},{1,12},{2,15},{3,14},{4,0},{5,1},{6,2},{7,3},{8,4},{9,5},{1... | collective-permute-start | bytes 786440 | tf_op jit(solution)/shard_map/ppermute | solution.py:43
  127.4 4.6 %collective-permute-done.12 = bf16[1024,128]{1,0:T(8,128)(2,1)S(1)} collective-permute-done((bf16[1024,128]{1,0:T(8,128)(2,1)S(1)}, bf16[1024,128]{1,0:T(8,128)(2,1)S(1)}, u32[]{:S(2)}, u32[]{:S(2)}) %collective-permute-start.12) | collective-permute-done | bytes 262176 | tf_op jit(solution)/shard_map/ppermute | solution.py:43
  132.1 1.9 %collective-permute-start.13 = (bf16[1024,128]{1,0:T(8,128)(2,1)S(1)}, bf16[1024,128]{1,0:T(8,128)(2,1)S(1)}, u32[]{:S(2)}, u32[]{:S(2)}) collective-permute-start(bf16[1024,128]{1,0:T(8,128)(2,1)S(1)} %get-tuple-element.15), channel_id=1, source_target_pairs={{0,4},{1,5},{2,6},{3,7},{4,8},{5,9},{6,10},{7,11},{8,12},{9,13},{1... | collective-permute-start | bytes 786440 | tf_op jit(solution)/shard_map/ppermute | solution.py:43
  134.0 1.4 collective-permute-start.16
  135.4 4.3 %collective-permute-done.13 = bf16[1024,128]{1,0:T(8,128)(2,1)S(1)} collective-permute-done((bf16[1024,128]{1,0:T(8,128)(2,1)S(1)}, bf16[1024,128]{1,0:T(8,128)(2,1)S(1)}, u32[]{:S(2)}, u32[]{:S(2)}) %collective-permute-start.13) | collective-permute-done | bytes 262176 | tf_op jit(solution)/shard_map/ppermute | solution.py:43
  140.5 12.6 %all_to_all.22 = bf16[16,64,128]{2,1,0:T(8,128)(2,1)S(1)} all-to-all(bf16[16,64,128]{2,1,0:T(8,128)(2,1)S(1)} %bitcast.18), channel_id=1, replica_groups={{0,16,32,48,64,80,96,112,128,144,160,176,192,208,224,240},{2,18,34,50,6..., dimensions={0} | all-to-all | bytes 524288 | tf_op jit(solution)/shard_map/all_to_all | solution.py:47
  (56 shorter events, 11.6 us)
Async XLA Ops:
  17.4 38.1 %copy-start.9 = (bf16[128,13]{0,1:T(8,128)(2,1)S(1)}, bf16[128,13]{0,1:T(8,128)(2,1)}, u32[]{:S(2)}) copy-start(bf16[128,13]{0,1:T(8,128)(2,1)} %param.12) | copy-start | bytes 9988
  17.5 49.0 %copy-start = (bf16[1792,512]{1,0:T(8,128)(2,1)S(1)}, bf16[1792,512]{1,0:T(8,128)(2,1)}, u32[]{:S(2)}) copy-start(bf16[1792,512]{1,0:T(8,128)(2,1)} %down_ref.1) | copy-start | bytes 5505028
  17.5 48.9 %copy-start.2 = (bf16[128,1792]{1,0:T(8,128)(2,1)S(1)}, bf16[128,1792]{1,0:T(8,128)(2,1)}, u32[]{:S(2)}) copy-start(bf16[128,1792]{1,0:T(8,128)(2,1)} %cot_ref.1) | copy-start | bytes 1376260
  17.5 48.9 %copy-start.3 = (bf16[512,256]{1,0:T(8,128)(2,1)S(1)}, bf16[512,256]{1,0:T(8,128)(2,1)}, u32[]{:S(2)}) copy-start(bf16[512,256]{1,0:T(8,128)(2,1)} %w2_ref.1) | copy-start | bytes 786436
  17.5 48.9 %copy-start.4 = (bf16[256,128]{1,0:T(8,128)(2,1)S(1)}, bf16[256,128]{1,0:T(8,128)(2,1)}, u32[]{:S(2)}) copy-start(bf16[256,128]{1,0:T(8,128)(2,1)} %w3_ref.1) | copy-start | bytes 196612
  17.5 48.9 %copy-start.5 = (bf16[13,512]{1,0:T(8,128)(2,1)S(1)}, bf16[13,512]{1,0:T(8,128)(2,1)}, u32[]{:S(2)}) copy-start(bf16[13,512]{1,0:T(8,128)(2,1)} %w1_ref.1) | copy-start | bytes 39940
  17.5 11.6 %collective-permute-start.3 = (bf16[1024,128]{1,0:T(8,128)(2,1)S(1)}, bf16[1024,128]{1,0:T(8,128)(2,1)S(1)}, u32[]{:S(2)}, u32[]{:S(2)}) collective-permute-start(bf16[1024,128]{1,0:T(8,128)(2,1)S(1)} %bitcast.12), channel_id=1, source_target_pairs={{0,4},{1,5},{2,6},{3,7},{4,8},{5,9},{6,10},{7,11},{8,12},{9,13},{1... | collective-permute-start | bytes 786440 | tf_op jit(solution)/shard_map/ppermute | solution.py:43
  19.5 12.7 %collective-permute-start = (bf16[1024,128]{1,0:T(8,128)(2,1)S(1)}, bf16[1024,128]{1,0:T(8,128)(2,1)S(1)}, u32[]{:S(2)}, u32[]{:S(2)}) collective-permute-start(bf16[1024,128]{1,0:T(8,128)(2,1)S(1)} %bitcast.13), channel_id=1, source_target_pairs={{0,13},{1,12},{2,15},{3,14},{4,0},{5,1},{6,2},{7,3},{8,4},{9,5},{1... | collective-permute-start | bytes 786440 | tf_op jit(solution)/shard_map/ppermute | solution.py:43
  23.6 10.0 %collective-permute-start.1 = (bf16[512,128]{1,0:T(8,128)(2,1)S(1)}, bf16[512,128]{1,0:T(8,128)(2,1)S(1)}, u32[]{:S(2)}, u32[]{:S(2)}) collective-permute-start(bf16[512,128]{1,0:T(8,128)(2,1)S(1)} %bitcast.20), channel_id=1, source_target_pairs={{0,9},{1,8},{2,11},{3,10},{4,13},{5,12},{6,15},{7,14},{8,0},{9,1},... | collective-permute-start | bytes 393224 | tf_op jit(solution)/shard_map/ppermute | solution.py:43
  26.0 8.2 %collective-permute-start.2 = (bf16[512,128]{1,0:T(8,128)(2,1)S(1)}, bf16[512,128]{1,0:T(8,128)(2,1)S(1)}, u32[]{:S(2)}, u32[]{:S(2)}) collective-permute-start(bf16[512,128]{1,0:T(8,128)(2,1)S(1)} %bitcast.19), channel_id=1, source_target_pairs={{0,8},{1,9},{2,10},{3,11},{4,12},{5,13},{6,14},{7,15},{8,1},{9,0},... | collective-permute-start | bytes 393224 | tf_op jit(solution)/shard_map/ppermute | solution.py:43
  26.6 7.7 %collective-permute-start.4 = (bf16[1024,128]{1,0:T(8,128)(2,1)S(1)}, bf16[1024,128]{1,0:T(8,128)(2,1)S(1)}, u32[]{:S(2)}, u32[]{:S(2)}) collective-permute-start(bf16[1024,128]{1,0:T(8,128)(2,1)S(1)} %bitcast.14), channel_id=1, source_target_pairs={{0,2},{2,0},{4,6},{6,4},{8,10},{10,8},{12,14},{14,12},{16,18},{18,... | collective-permute-start | bytes 786440 | tf_op jit(solution)/shard_map/ppermute | solution.py:243
  29.1 6.5 %collective-permute-start.8 = (bf16[1024,128]{1,0:T(8,128)(2,1)S(1)}, bf16[1024,128]{1,0:T(8,128)(2,1)S(1)}, u32[]{:S(2)}, u32[]{:S(2)}) collective-permute-start(bf16[1024,128]{1,0:T(8,128)(2,1)S(1)} %collective-permute-done.3.refs_4_), channel_id=1, source_target_pairs={{0,2},{2,0},{4,6},{6,4},{8,10},{10,8},{12,14},{14,12},{16,18},{18,... | collective-permute-start | bytes 786440 | tf_op jit(solution)/shard_map/ppermute | solution.py:243
  32.2 3.4 %collective-permute-start.5 = (bf16[1024,128]{1,0:T(8,128)(2,1)S(1)}, bf16[1024,128]{1,0:T(8,128)(2,1)S(1)}, u32[]{:S(2)}, u32[]{:S(2)}) collective-permute-start(bf16[1024,128]{1,0:T(8,128)(2,1)S(1)} %collective-permute-done.refs_1_), channel_id=1, source_target_pairs={{0,2},{2,0},{4,6},{6,4},{8,10},{10,8},{12,14},{14,12},{16,18},{18,... | collective-permute-start | bytes 786440 | tf_op jit(solution)/shard_map/ppermute | solution.py:243
  33.6 1.3 collective-permute-start.6
  34.2 1.3 collective-permute-start.7
  50.8 15.6 %all-to-all-start.1 = ((bf16[16,128,128]{2,1,0:T(8,128)(2,1)}), bf16[16,128,128]{2,1,0:T(8,128)(2,1)S(1)}, u32[]{:S(2)}, u32[]{:S(2)}) async-start(bf16[16,128,128]{2,1,0:T(8,128)(2,1)} %bitcast.6), calls=%async_computation.1 | async-start | bytes 1048576 | tf_op jit(solution)/shard_map/all_to_all | solution.py:47
  102.2 2.7 %collective-permute-start.9 = (bf16[4096,128]{1,0:T(8,128)(2,1)S(1)}, bf16[4096,128]{1,0:T(8,128)(2,1)S(1)}, u32[]{:S(2)}, u32[]{:S(2)}) collective-permute-start(bf16[4096,128]{1,0:T(8,128)(2,1)S(1)} %get-tuple-element.10), channel_id=1, source_target_pairs={{0,2},{2,0},{4,6},{6,4},{8,10},{10,8},{12,14},{14,12},{16,18},{18,... | collective-permute-start | bytes 3145736 | tf_op jit(solution)/shard_map/ppermute | solution.py:252
  105.2 9.8 %collective-permute-start.10 = (bf16[1024,128]{1,0:T(8,128)(2,1)S(1)}, bf16[1024,128]{1,0:T(8,128)(2,1)S(1)}, u32[]{:S(2)}, u32[]{:S(2)}) collective-permute-start(bf16[1024,128]{1,0:T(8,128)(2,1)S(1)} %get-tuple-element.19), channel_id=1, source_target_pairs={{0,4},{1,5},{2,6},{3,7},{4,8},{5,9},{6,10},{7,11},{8,12},{9,13},{1... | collective-permute-start | bytes 786440 | tf_op jit(solution)/shard_map/ppermute | solution.py:43
  107.3 10.2 %collective-permute-start.14 = (bf16[1024,128]{1,0:T(8,128)(2,1)S(1)}, bf16[1024,128]{1,0:T(8,128)(2,1)S(1)}, u32[]{:S(2)}, u32[]{:S(2)}) collective-permute-start(bf16[1024,128]{1,0:T(8,128)(2,1)S(1)} %get-tuple-element.20), channel_id=1, source_target_pairs={{0,13},{1,12},{2,15},{3,14},{4,0},{5,1},{6,2},{7,3},{8,4},{9,5},{1... | collective-permute-start | bytes 786440 | tf_op jit(solution)/shard_map/ppermute | solution.py:43
  115.1 8.8 %collective-permute-start.11 = (bf16[1024,128]{1,0:T(8,128)(2,1)S(1)}, bf16[1024,128]{1,0:T(8,128)(2,1)S(1)}, u32[]{:S(2)}, u32[]{:S(2)}) collective-permute-start(bf16[1024,128]{1,0:T(8,128)(2,1)S(1)} %add_convert_fusion.5), channel_id=1, source_target_pairs={{0,4},{1,5},{2,6},{3,7},{4,8},{5,9},{6,10},{7,11},{8,12},{9,13},{1... | collective-permute-start | bytes 786440 | tf_op jit(solution)/shard_map/ppermute | solution.py:43
  124.0 7.9 %collective-permute-start.12 = (bf16[1024,128]{1,0:T(8,128)(2,1)S(1)}, bf16[1024,128]{1,0:T(8,128)(2,1)S(1)}, u32[]{:S(2)}, u32[]{:S(2)}) collective-permute-start(bf16[1024,128]{1,0:T(8,128)(2,1)S(1)} %get-tuple-element.17), channel_id=1, source_target_pairs={{0,4},{1,5},{2,6},{3,7},{4,8},{5,9},{6,10},{7,11},{8,12},{9,13},{1... | collective-permute-start | bytes 786440 | tf_op jit(solution)/shard_map/ppermute | solution.py:43
  124.9 7.1 %collective-permute-start.15 = (bf16[1024,128]{1,0:T(8,128)(2,1)S(1)}, bf16[1024,128]{1,0:T(8,128)(2,1)S(1)}, u32[]{:S(2)}, u32[]{:S(2)}) collective-permute-start(bf16[1024,128]{1,0:T(8,128)(2,1)S(1)} %get-tuple-element.18), channel_id=1, source_target_pairs={{0,13},{1,12},{2,15},{3,14},{4,0},{5,1},{6,2},{7,3},{8,4},{9,5},{1... | collective-permute-start | bytes 786440 | tf_op jit(solution)/shard_map/ppermute | solution.py:43
  132.1 7.7 %collective-permute-start.13 = (bf16[1024,128]{1,0:T(8,128)(2,1)S(1)}, bf16[1024,128]{1,0:T(8,128)(2,1)S(1)}, u32[]{:S(2)}, u32[]{:S(2)}) collective-permute-start(bf16[1024,128]{1,0:T(8,128)(2,1)S(1)} %get-tuple-element.15), channel_id=1, source_target_pairs={{0,4},{1,5},{2,6},{3,7},{4,8},{5,9},{6,10},{7,11},{8,12},{9,13},{1... | collective-permute-start | bytes 786440 | tf_op jit(solution)/shard_map/ppermute | solution.py:43
  134.0 6.4 %collective-permute-start.16 = (bf16[1024,128]{1,0:T(8,128)(2,1)S(1)}, bf16[1024,128]{1,0:T(8,128)(2,1)S(1)}, u32[]{:S(2)}, u32[]{:S(2)}) collective-permute-start(bf16[1024,128]{1,0:T(8,128)(2,1)S(1)} %get-tuple-element.16), channel_id=1, source_target_pairs={{0,13},{1,12},{2,15},{3,14},{4,0},{5,1},{6,2},{7,3},{8,4},{9,5},{1... | collective-permute-start | bytes 786440 | tf_op jit(solution)/shard_map/ppermute | solution.py:43
  (4 other events, 97.8 us)

commit v2 on v1

--- a/solution.py
+++ b/solution.py
@@ -25,6 +25,7 @@
 ROWS = CORES * HALF
 
 across = [[g * COLUMN + k for g in range(GROUPS)] for k in range(COLUMN)]
+across_reps = [[d * REPS + r for d in group for r in range(REPS)] for group in across]
 swap_cores = [(s, s ^ 1) for s in range(SHARDS)]
 
 
@@ -33,7 +34,7 @@
     for s in range(SHARDS):
         place, z_lo, core = s // COLUMN, (s // CORES) % Z_LO, s % CORES
         for r in range(REPS):
-            z = (r * Z_LO + z_lo + step) % Z
+            z = (r * Z_LO + z_lo + (step if core == 0 else -step)) % Z
             target = place * COLUMN + (z % Z_LO) * CORES + core
             pairs.append((s * REPS + r, target * REPS + z // Z_LO))
     return pairs
@@ -43,19 +44,34 @@
     return lax.ppermute(x, ("shard", "rep"), along_z(step))
 
 
+def swap(x):
+    return lax.ppermute(x, "shard", swap_cores)
+
+
 def exchange(x):
     return lax.all_to_all(
         x, "shard", split_axis=0, concat_axis=0, axis_index_groups=across, tiled=True
     )
 
 
+def exchange_reps(x):
+    return lax.all_to_all(
+        x,
+        ("shard", "rep"),
+        split_axis=0,
+        concat_axis=0,
+        axis_index_groups=across_reps,
+        tiled=True,
+    )
+
+
 vmem = pl.BlockSpec(memory_space=pltpu.VMEM)
 smem = pl.BlockSpec(memory_space=pltpu.SMEM)
 
 
-def lookup(ids, parts, unroll=32):
+def lookup(ids, parts, samples, unroll=32):
     count = len(parts)
-    places, samples = GROUPS, ids.shape[1]
+    places = GROUPS
 
     def body(ids_ref, *refs):
         part_refs, (out_ref, tab, acc) = refs[:count], refs[count:]
@@ -67,10 +83,13 @@
 
         def place(g, _):
             def some(i, _):
+                base = g * (POOL * samples) + i * unroll
+                bag = g * samples + i * unroll
                 for u in range(unroll):
-                    s = i * unroll + u
-                    r = [tab[pl.ds(ids_ref[g * POOL + j, s], 1), :] for j in range(POOL)]
-                    acc[pl.ds(g * samples + s, 1), :] = (r[0] + r[1]) + (r[2] + r[3])
+                    r = [
+                        tab[pl.ds(ids_ref[base + (j * samples + u)], 1), :] for j in range(POOL)
+                    ]
+                    acc[pl.ds(bag + u, 1), :] = (r[0] + r[1]) + (r[2] + r[3])
                 return 0
 
             return lax.fori_loop(0, samples // unroll, some, 0)
@@ -87,40 +106,50 @@
             pltpu.VMEM((ROWS + 8, EMB), f32),
             pltpu.VMEM((places * samples, EMB), f32),
         ],
-        compiler_params=pltpu.CompilerParams(vmem_limit_bytes=40 << 20),
+        compiler_params=pltpu.CompilerParams(vmem_limit_bytes=24 << 20),
         name="lookup",
     )(ids, *parts)
 
 
-def scatter(ids, grads, unroll=16):
-    places, samples = GROUPS, ids.shape[1]
-
-    def body(ids_ref, grads_ref, keep_ref, send_ref, a0, a1, a2, a3, wide):
-        accs = (a0, a1, a2, a3)
+def scatter(ids, grads, samples, unroll=16):
+    places, pair = GROUPS, 2
+    totals = pair * POOL
+
+    def body(ids_ref, grads_ref, keep_ref, send_ref, *scratch):
+        accs, wide = scratch[:totals], scratch[totals]
         for a in accs:
             a[...] = jnp.zeros((ROWS + 8, EMB), f32)
         wide[...] = grads_ref[...].astype(f32)
 
         def place(g, _):
             def some(i, _):
-                for u in range(unroll):
-                    s = i * unroll + u
-                    row = wide[pl.ds(g * samples + s, 1), :]
-                    at = [ids_ref[g * POOL + j, s] for j in range(POOL)]
-                    v = [accs[j][pl.ds(at[j], 1), :] for j in range(POOL)]
-                    v = [x + row for x in v]
-                    for j in range(POOL):
-                        accs[j][pl.ds(at[j], 1), :] = v[j]
+                base = g * (POOL * samples) + i * unroll
+                bag = g * samples + i * unroll
+                for u in range(0, unroll, pair):
+                    row = [wide[pl.ds(bag + (u + k), 1), :] for k in range(pair)]
+                    at = [
+                        ids_ref[base + (j * samples + u + k)]
+                        for k in range(pair)
+                        for j in range(POOL)
+                    ]
+                    new = [
+                        accs[n][pl.ds(at[n], 1), :] + row[n // POOL] for n in range(totals)
+                    ]
+                    for n in range(totals):
+                        accs[n][pl.ds(at[n], 1), :] = new[n]
                 return 0
 
             return lax.fori_loop(0, samples // unroll, some, 0)
 
         lax.fori_loop(0, places, place, 0)
-        block = 512
+        block = 256
 
         def total(at):
             sl = pl.ds(pl.multiple_of(at, block), block)
-            return (a0[sl, :] + a1[sl, :]) + (a2[sl, :] + a3[sl, :])
+            t = [a[sl, :] for a in accs]
+            while len(t) > 1:
+                t = [t[2 * k] + t[2 * k + 1] for k in range(len(t) // 2)]
+            return t[0]
 
         def finish(i, _):
             sl = pl.ds(pl.multiple_of(i * block, block), block)
@@ -138,9 +167,9 @@
         ],
         in_specs=[smem, vmem],
         out_specs=[vmem, vmem],
-        scratch_shapes=[pltpu.VMEM((ROWS + 8, EMB), f32)] * POOL
+        scratch_shapes=[pltpu.VMEM((ROWS + 8, EMB), f32)] * totals
         + [pltpu.VMEM((places * samples, EMB), f32)],
-        compiler_params=pltpu.CompilerParams(vmem_limit_bytes=50 << 20),
+        compiler_params=pltpu.CompilerParams(vmem_limit_bytes=44 << 20),
         name="scatter",
     )(ids, grads)
 
@@ -193,7 +222,7 @@
         in_specs=[vmem] * 9,
         out_specs=[vmem, vmem],
         scratch_shapes=[pltpu.VMEM((rows, width), bf16)],
-        compiler_params=pltpu.CompilerParams(vmem_limit_bytes=40 << 20),
+        compiler_params=pltpu.CompilerParams(vmem_limit_bytes=20 << 20),
         name="cross",
     )(dense, w1, w2, w3, pooled, down, up, bias.reshape(1, width), cot)
 
@@ -220,9 +249,8 @@
     used = jnp.arange(pool, dtype=i32)[None, :, None] < bag_lengths.T[:, None, :]
     owner, row = ids >> 6, ids & 63
     place, owner_z, owner_core = owner >> 3, (owner >> 1) & 3, owner & 1
-    address = (
-        (owner_core ^ my_core) * HALF + ((owner_z - my_z) & 3) * PIECE + place * ROWS_DEV + row
-    )
+    steps = ((owner_z - my_z) * (1 - 2 * my_core)) & 3
+    address = (owner_core ^ my_core) * HALF + steps * PIECE + place * ROWS_DEV + row
     address = jnp.where(used, address, ROWS)
     digits = jnp.concatenate([address >> 7, address & 127], axis=1).astype(f32).astype(bf16)
     payload = jnp.concatenate([tables, digits], axis=1)
@@ -230,37 +258,34 @@
     got = exchange(payload)
     own = got[:, :ROWS_DEV].reshape(PIECE, EMB)
     high, low = got[:, ROWS_DEV : ROWS_DEV + pool], got[:, ROWS_DEV + pool :]
-    at = (high.astype(f32) * 128.0 + low.astype(f32)).astype(i32).reshape(GROUPS * pool, samples)
-
-    mid = PIECE // 2
-    pieces = [
-        own,
-        send_z(own, -1),
-        send_z(own[:mid], -2),
-        send_z(own[mid:], 2),
-        send_z(own, 1),
-    ]
-    others = [lax.ppermute(x, "shard", swap_cores) for x in pieces]
-    pooled = exchange(lookup(at, pieces + others).reshape(GROUPS, samples, EMB))
+    at = (high.astype(f32) * 128.0 + low.astype(f32)).astype(i32).reshape(-1)
+
+    two = send_z(own, -2)
+    one, three = send_z(own, -1), send_z(own, 1)
+    pieces = [own, one, two, three] + [swap(x) for x in (own, three, two, one)]
+    pooled = exchange(lookup(at, pieces, samples).reshape(GROUPS, samples, EMB))
 
     crossed, pooled_grad = cross(
         dense_feats, bottom_w1, bottom_w2, bottom_w3, pooled, cross_down, cross_up, cross_bias,
         cotangent,
     )
     grads = exchange(pooled_grad).reshape(GROUPS * samples, EMB)
-    keep, send = scatter(at, grads)
-    both = keep + lax.ppermute(send, "shard", swap_cores).astype(f32)
-    part = [both[d * PIECE : (d + 1) * PIECE] for d in range(Z_LO)]
-
-    up, dn = part[0], part[1]
-    for d in (3, 2, 1):
-        up = send_z(up.astype(bf16), 1).astype(f32) + part[d]
-    up = send_z(up.astype(bf16), 1).astype(f32)
-    for d in (2, 3):
-        dn = send_z(dn.astype(bf16), -1).astype(f32) + part[d]
-    dn = send_z(dn.astype(bf16), -1).astype(f32)
-    summed = (part[0] + up + dn).astype(bf16).reshape(GROUPS, ROWS_DEV, EMB)
-    row_grad = exchange(summed)[:table_count].astype(f32)
+    keep, send = scatter(at, grads, samples)
+    theirs = swap(send).reshape(Z_LO, PIECE, EMB)
+    keep = keep.reshape(Z_LO, PIECE, EMB)
+
+    def chip(d):
+        return keep[d] + theirs[-d % Z_LO].astype(f32)
+
+    far = send_z(chip(2).astype(bf16), -1)
+    below = send_z(chip(1).astype(bf16), 1)
+    above = send_z((chip(3) + far.astype(f32)).astype(bf16), -1)
+    summed = (chip(0) + below.astype(f32) + above.astype(f32)).astype(bf16)
+    summed = summed.reshape(GROUPS, 1, ROWS_DEV, EMB)
+    halves = exchange_reps(
+        jnp.broadcast_to(summed, (GROUPS, REPS, ROWS_DEV, EMB)).reshape(-1, ROWS_DEV, EMB)
+    ).reshape(GROUPS, REPS, ROWS_DEV, EMB)[:table_count]
+    row_grad = halves.astype(f32).sum(axis=1)
     new_accum = accum + jnp.mean(row_grad * row_grad, axis=2)
     new_tables = tables.astype(f32) - step_size * row_grad / (
         jnp.sqrt(new_accum)[:, :, None] + adagrad_eps

time: 157 us -> 142 us (0.904)
  waiting for transfers between devices: 44.9 us -> 31.6 us
  blocking collectives: 41.5 us -> 54.1 us
  Pallas kernels: 35.4 us -> 25.6 us
  starting transfers between devices: 26.1 us -> 22.2 us
    all_to_all x0 -> x1, blocking collectives: none -> 24.9 us  [exchange_reps(): lax.all_to_all(x, ('shard', 'rep'), split_axis=0, concat_axis=0, axis_ind...]
    ppermute x11 -> x6, waiting for transfers between devices: 30.3 us -> 16.9 us  [send_z(): return lax.ppermute(x, ('shard', 'rep'), along_z(step))]
    all_to_all x3 -> x2, blocking collectives: 41.5 us -> 29.2 us  [exchange(): lax.all_to_all(x, 'shard', split_axis=0, concat_axis=0, axis_index_groups...]
    pallas_call x1, Pallas kernels: 15.2 us -> 9.21 us  [lookup(): pl.pallas_call(body, out_shape=jax.ShapeDtypeStruct((places * samples, EM...]
    ppermute x11 -> x6, starting transfers between devices: 21.2 us -> 15.5 us  [send_z(): return lax.ppermute(x, ('shard', 'rep'), along_z(step))]
    pallas_call x1, Pallas kernels: 17.1 us -> 13.3 us  [scatter(): pl.pallas_call(body, out_shape=[jax.ShapeDtypeStruct((HALF, EMB), f32), j...]
    ppermute x6 -> x5, starting transfers between devices: 0.11 us -> 1.87 us  [swap(): return lax.ppermute(x, 'shard', swap_cores)]
    ppermute x6 -> x5, waiting for transfers between devices: 3.97 us -> 3.77 us  [swap(): return lax.ppermute(x, 'shard', swap_cores)]
  transfers between devices with their start and end apart: 18 -> 12, of which waited for: 15 -> 8; matrix products, arithmetic and copies ran while one was open for 0% -> 0% of each run, Pallas kernels for 0% -> 0%
where the time goes in v2:
time: 142 us; the launch traced here: 140 us
  blocking collectives  54.1 us (38%)
  waiting for transfers between devices  31.6 us (22%)
  Pallas kernels  25.6 us (18%)
  starting transfers between devices  22.2 us (16%)
  other arithmetic  3.94 us (3%)
  local copies, waits for them, and re-layouts  1.84 us (1%)
    all_to_all x2, blocking collectives, exchange(): lax.all_to_all(x, 'shard', split_axis=0, concat_axis=0, axis_index_groups...  29.2 us
    all_to_all x1, blocking collectives, exchange_reps(): lax.all_to_all(x, ('shard', 'rep'), split_axis=0, concat_axis=0, axis_ind...  24.9 us
    ppermute x6, waiting for transfers between devices, send_z(): return lax.ppermute(x, ('shard', 'rep'), along_z(step))  16.9 us
    ppermute x6, starting transfers between devices, send_z(): return lax.ppermute(x, ('shard', 'rep'), along_z(step))  15.5 us
    pallas_call x1, Pallas kernels, scatter(): pl.pallas_call(body, out_shape=[jax.ShapeDtypeStruct((HALF, EMB), f32), j...  13.3 us
    all_to_all x1, waiting for transfers between devices, exchange(): lax.all_to_all(x, 'shard', split_axis=0, concat_axis=0, axis_index_groups...  10.8 us
    pallas_call x1, Pallas kernels, lookup(): pl.pallas_call(body, out_shape=jax.ShapeDtypeStruct((places * samples, EM...  9.21 us
    all_to_all x1, starting transfers between devices, exchange(): lax.all_to_all(x, 'shard', split_axis=0, concat_axis=0, axis_index_groups...  4.82 us
  transfers between devices with their start and end apart: 12, of which 8 were waited for; matrix products, arithmetic and copies ran while one was open for 0% of the time, Pallas kernels for 0%

profile of v2, /device:TPU:2, one launch (start us, length us, event | category | flops | bytes accessed | tf_op | source)
XLA Modules:
  0.0 140.1 jit_solution(11067386211854420783)
XLA Ops:
  0.7 0.8 broadcast_shift-right-arithmetic_fusion
  1.5 1.0 fusion.2
  2.5 14.9 %all_to_all.20 = bf16[16,72,128]{2,1,0:T(8,128)(2,1)S(1)} all-to-all(bf16[16,72,128]{2,1,0:T(8,128)(2,1)S(1)} %fusion.2), channel_id=1, replica_groups={{0,16,32,48,64,80,96,112,128,144,160,176,192,208,224,240},{2,18,34,50,6..., dimensions={0} | all-to-all | bytes 589824 | tf_op jit(solution)/shard_map/all_to_all | solution.py:52
  17.5 2.0 %collective-permute-start.2 = (bf16[1024,128]{1,0:T(8,128)(2,1)S(1)}, bf16[1024,128]{1,0:T(8,128)(2,1)S(1)}, u32[]{:S(2)}, u32[]{:S(2)}) collective-permute-start(bf16[1024,128]{1,0:T(8,128)(2,1)S(1)} %bitcast.13), channel_id=1, source_target_pairs={{0,4},{1,5},{2,15},{3,14},{4,8},{5,9},{6,2},{7,3},{8,12},{9,13},{1... | collective-permute-start | bytes 786440 | tf_op jit(solution)/shard_map/ppermute | solution.py:44
  19.5 5.4 %collective-permute-start.1 = (bf16[1024,128]{1,0:T(8,128)(2,1)S(1)}, bf16[1024,128]{1,0:T(8,128)(2,1)S(1)}, u32[]{:S(2)}, u32[]{:S(2)}) collective-permute-start(bf16[1024,128]{1,0:T(8,128)(2,1)S(1)} %bitcast.14), channel_id=1, source_target_pairs={{0,9},{1,8},{2,10},{3,11},{4,13},{5,12},{6,14},{7,15},{8,0},{9,1},... | collective-permute-start | bytes 786440 | tf_op jit(solution)/shard_map/ppermute | solution.py:44
  24.9 1.0 collective-permute-start
  25.9 6.9 %collective-permute-done.2.refs_3_ = bf16[1024,128]{1,0:T(8,128)(2,1)S(1)} collective-permute-done((bf16[1024,128]{1,0:T(8,128)(2,1)S(1)}, bf16[1024,128]{1,0:T(8,128)(2,1)S(1)}, u32[]{:S(2)}, u32[]{:S(2)}) %collective-permute-start.2) | collective-permute-done | bytes 262176 | tf_op jit(solution)/shard_map/ppermute | solution.py:44
  32.8 1.4 collective-permute-start.5
  34.8 0.6 collective-permute-done.5.refs_6_
  35.9 9.2 %lookup.1 = bf16[2048,128]{1,0:T(8,128)(2,1)} custom-call(s32[8192]{0:T(1024)S(1)} %bitcast.18, bf16[1024,128]{1,0:T(8,128)(2,1)S(1)} %bitcast.17, bf16[1024,128]{1,0:T(8,128)(2,1)S(1)} %collective-permute-done.refs_1_, bf16[1024,128]{1,0:T(8,128)(2,1)S(1)} %collective-permute-done.1.refs_2_, bf16[1024,128]{1,0:T(8,128)(2,1)S(1)} %collective-permute-done.2.refs_3_, ...), custom_call_target="tpu_custom_call" | custom-call | tf_op jit(solution)/shard_map/lookup/pallas_call | solution.py:100
  45.1 4.8 %all-to-all-start.1 = ((bf16[16,128,128]{2,1,0:T(8,128)(2,1)}), bf16[16,128,128]{2,1,0:T(8,128)(2,1)S(1)}, u32[]{:S(2)}, u32[]{:S(2)}) async-start(bf16[16,128,128]{2,1,0:T(8,128)(2,1)} %bitcast.4), calls=%async_computation.1 | async-start | bytes 1048576 | tf_op jit(solution)/shard_map/all_to_all | solution.py:52
  50.1 10.8 %all-to-all-done.1.pooled_ref = bf16[16,128,128]{2,1,0:T(8,128)(2,1)S(1)} async-done(((bf16[16,128,128]{2,1,0:T(8,128)(2,1)}), bf16[16,128,128]{2,1,0:T(8,128)(2,1)S(1)}, u32[]{:S(2)}, u32[]{:S(2)}) %all-to-all-start.1) | async-done | bytes 524320 | tf_op jit(solution)/shard_map/all_to_all | solution.py:52
  61.0 1.5 %copy-done.1 = bf16[512,1792]{1,0:T(8,128)(2,1)S(1)} copy-done((bf16[512,1792]{1,0:T(8,128)(2,1)S(1)}, bf16[512,1792]{1,0:T(8,128)(2,1)}, u32[]{:S(2)}) %copy-start.1) | copy-done | bytes 1835032
  62.5 3.1 %cross.1 = (bf16[128,1792]{1,0:T(8,128)(2,1)}, bf16[16,128,128]{2,1,0:T(8,128)(2,1)S(1)}) custom-call(bf16[128,13]{1,0:T(8,128)(2,1)S(1)} %copy.16.dense_ref, bf16[13,512]{1,0:T(8,128)(2,1)S(1)} %copy-done.5, bf16[512,256]{1,0:T(8,128)(2,1)S(1)} %copy-done.3, bf16[256,128]{1,0:T(8,128)(2,1)S(1)} %copy-done.4, ...), custom_call_target="tpu_custom_call" | custom-call | tf_op jit(solution)/shard_map/cross/pallas_call | solution.py:216
  65.6 14.2 %all_to_all.21 = bf16[16,128,128]{2,1,0:T(8,128)(2,1)S(1)} all-to-all(bf16[16,128,128]{2,1,0:T(8,128)(2,1)S(1)} %get-tuple-element.8), channel_id=1, replica_groups={{0,16,32,48,64,80,96,112,128,144,160,176,192,208,224,240},{2,18,34,50,6..., dimensions={0} | all-to-all | bytes 1048576 | tf_op jit(solution)/shard_map/all_to_all | solution.py:52
  79.8 13.3 %scatter.1 = (f32[4096,128]{1,0:T(8,128)S(1)}, bf16[4096,128]{1,0:T(8,128)(2,1)S(1)}) custom-call(s32[8192]{0:T(1024)S(1)} %bitcast.19, bf16[2048,128]{1,0:T(8,128)(2,1)S(1)} %bitcast.12), custom_call_target="tpu_custom_call" | custom-call | tf_op jit(solution)/shard_map/scatter/pallas_call | solution.py:162
  93.2 2.6 %collective-permute-done.7 = bf16[4096,128]{1,0:T(8,128)(2,1)S(1)} collective-permute-done((bf16[4096,128]{1,0:T(8,128)(2,1)S(1)}, bf16[4096,128]{1,0:T(8,128)(2,1)S(1)}, u32[]{:S(2)}, u32[]{:S(2)}) %collective-permute-start.7) | collective-permute-done | bytes 1048608 | tf_op jit(solution)/shard_map/ppermute | solution.py:48
  96.0 3.4 %collective-permute-start.9 = (bf16[1024,128]{1,0:T(8,128)(2,1)S(1)}, bf16[1024,128]{1,0:T(8,128)(2,1)S(1)}, u32[]{:S(2)}, u32[]{:S(2)}) collective-permute-start(bf16[1024,128]{1,0:T(8,128)(2,1)S(1)} %get-tuple-element.16), channel_id=1, source_target_pairs={{0,13},{1,12},{2,6},{3,7},{4,0},{5,1},{6,10},{7,11},{8,4},{9,5},{1... | collective-permute-start | bytes 786440 | tf_op jit(solution)/shard_map/ppermute | solution.py:44
  99.3 6.0 %collective-permute-done.9 = bf16[1024,128]{1,0:T(8,128)(2,1)S(1)} collective-permute-done((bf16[1024,128]{1,0:T(8,128)(2,1)S(1)}, bf16[1024,128]{1,0:T(8,128)(2,1)S(1)}, u32[]{:S(2)}, u32[]{:S(2)}) %collective-permute-start.9) | collective-permute-done | bytes 262176 | tf_op jit(solution)/shard_map/ppermute | solution.py:44
  105.4 3.8 %collective-permute-start.10 = (bf16[1024,128]{1,0:T(8,128)(2,1)S(1)}, bf16[1024,128]{1,0:T(8,128)(2,1)S(1)}, u32[]{:S(2)}, u32[]{:S(2)}) collective-permute-start(bf16[1024,128]{1,0:T(8,128)(2,1)S(1)} %add_convert_fusion.1), channel_id=1, source_target_pairs={{0,13},{1,12},{2,6},{3,7},{4,0},{5,1},{6,10},{7,11},{8,4},{9,5},{1... | collective-permute-start | bytes 786440 | tf_op jit(solution)/shard_map/ppermute | solution.py:44
  109.2 3.9 %collective-permute-done.10 = bf16[1024,128]{1,0:T(8,128)(2,1)S(1)} collective-permute-done((bf16[1024,128]{1,0:T(8,128)(2,1)S(1)}, bf16[1024,128]{1,0:T(8,128)(2,1)S(1)}, u32[]{:S(2)}, u32[]{:S(2)}) %collective-permute-start.10) | collective-permute-done | bytes 262176 | tf_op jit(solution)/shard_map/ppermute | solution.py:44
  113.3 24.9 %all_to_all.22 = bf16[32,64,128]{2,1,0:T(8,128)(2,1)S(1)} all-to-all(bf16[32,64,128]{2,1,0:T(8,128)(2,1)S(1)} %bitcast.20), channel_id=1, replica_groups={{0,1,16,17,32,33,48,49,64,65,80,81,96,97,112,113,128,129,144,145,160,16..., dimensions={0} | all-to-all | bytes 1048576 | tf_op jit(solution)/shard_map/all_to_all | solution.py:58
  138.5 0.6 sqrt_add_fusion
  139.1 0.9 divide_subtract_fusion
  (43 shorter events, 2.2 us)
Async XLA Ops:
  17.4 32.5 %copy-start.7 = (f32[1792]{0:T(1024)S(1)}, f32[1792]{0:T(1024)}, u32[]{:S(2)}) copy-start(f32[1792]{0:T(1024)} %param.22) | copy-start | bytes 21508
  17.4 32.6 %copy-start.9 = (bf16[128,13]{0,1:T(8,128)(2,1)S(1)}, bf16[128,13]{0,1:T(8,128)(2,1)}, u32[]{:S(2)}) copy-start(bf16[128,13]{0,1:T(8,128)(2,1)} %param.12) | copy-start | bytes 9988
  17.4 43.6 %copy-start = (bf16[1792,512]{1,0:T(8,128)(2,1)S(1)}, bf16[1792,512]{1,0:T(8,128)(2,1)}, u32[]{:S(2)}) copy-start(bf16[1792,512]{1,0:T(8,128)(2,1)} %down_ref.1) | copy-start | bytes 5505028
  17.4 43.6 %copy-start.2 = (bf16[128,1792]{1,0:T(8,128)(2,1)S(1)}, bf16[128,1792]{1,0:T(8,128)(2,1)}, u32[]{:S(2)}) copy-start(bf16[128,1792]{1,0:T(8,128)(2,1)} %cot_ref.1) | copy-start | bytes 1376260
  17.4 43.6 %copy-start.3 = (bf16[512,256]{1,0:T(8,128)(2,1)S(1)}, bf16[512,256]{1,0:T(8,128)(2,1)}, u32[]{:S(2)}) copy-start(bf16[512,256]{1,0:T(8,128)(2,1)} %w2_ref.1) | copy-start | bytes 786436
  17.4 43.5 %copy-start.4 = (bf16[256,128]{1,0:T(8,128)(2,1)S(1)}, bf16[256,128]{1,0:T(8,128)(2,1)}, u32[]{:S(2)}) copy-start(bf16[256,128]{1,0:T(8,128)(2,1)} %w3_ref.1) | copy-start | bytes 196612
  17.4 43.5 %copy-start.5 = (bf16[13,512]{1,0:T(8,128)(2,1)S(1)}, bf16[13,512]{1,0:T(8,128)(2,1)}, u32[]{:S(2)}) copy-start(bf16[13,512]{1,0:T(8,128)(2,1)} %w1_ref.1) | copy-start | bytes 39940
  17.5 15.3 %collective-permute-start.2 = (bf16[1024,128]{1,0:T(8,128)(2,1)S(1)}, bf16[1024,128]{1,0:T(8,128)(2,1)S(1)}, u32[]{:S(2)}, u32[]{:S(2)}) collective-permute-start(bf16[1024,128]{1,0:T(8,128)(2,1)S(1)} %bitcast.13), channel_id=1, source_target_pairs={{0,4},{1,5},{2,15},{3,14},{4,8},{5,9},{6,2},{7,3},{8,12},{9,13},{1... | collective-permute-start | bytes 786440 | tf_op jit(solution)/shard_map/ppermute | solution.py:44
  19.5 13.3 %collective-permute-start.1 = (bf16[1024,128]{1,0:T(8,128)(2,1)S(1)}, bf16[1024,128]{1,0:T(8,128)(2,1)S(1)}, u32[]{:S(2)}, u32[]{:S(2)}) collective-permute-start(bf16[1024,128]{1,0:T(8,128)(2,1)S(1)} %bitcast.14), channel_id=1, source_target_pairs={{0,9},{1,8},{2,10},{3,11},{4,13},{5,12},{6,14},{7,15},{8,0},{9,1},... | collective-permute-start | bytes 786440 | tf_op jit(solution)/shard_map/ppermute | solution.py:44
  24.9 9.5 %collective-permute-start = (bf16[1024,128]{1,0:T(8,128)(2,1)S(1)}, bf16[1024,128]{1,0:T(8,128)(2,1)S(1)}, u32[]{:S(2)}, u32[]{:S(2)}) collective-permute-start(bf16[1024,128]{1,0:T(8,128)(2,1)S(1)} %bitcast.15), channel_id=1, source_target_pairs={{0,13},{1,12},{2,6},{3,7},{4,0},{5,1},{6,10},{7,11},{8,4},{9,5},{1... | collective-permute-start | bytes 786440 | tf_op jit(solution)/shard_map/ppermute | solution.py:44
  25.9 8.9 %collective-permute-start.3 = (bf16[1024,128]{1,0:T(8,128)(2,1)S(1)}, bf16[1024,128]{1,0:T(8,128)(2,1)S(1)}, u32[]{:S(2)}, u32[]{:S(2)}) collective-permute-start(bf16[1024,128]{1,0:T(8,128)(2,1)S(1)} %bitcast.16), channel_id=1, source_target_pairs={{0,2},{2,0},{4,6},{6,4},{8,10},{10,8},{12,14},{14,12},{16,18},{18,... | collective-permute-start | bytes 786440 | tf_op jit(solution)/shard_map/ppermute | solution.py:48
  32.8 2.0 %collective-permute-start.4 = (bf16[1024,128]{1,0:T(8,128)(2,1)S(1)}, bf16[1024,128]{1,0:T(8,128)(2,1)S(1)}, u32[]{:S(2)}, u32[]{:S(2)}) collective-permute-start(bf16[1024,128]{1,0:T(8,128)(2,1)S(1)} %collective-permute-done.2.refs_3_), channel_id=1, source_target_pairs={{0,2},{2,0},{4,6},{6,4},{8,10},{10,8},{12,14},{14,12},{16,18},{18,... | collective-permute-start | bytes 786440 | tf_op jit(solution)/shard_map/ppermute | solution.py:48
  32.8 2.6 %collective-permute-start.5 = (bf16[1024,128]{1,0:T(8,128)(2,1)S(1)}, bf16[1024,128]{1,0:T(8,128)(2,1)S(1)}, u32[]{:S(2)}, u32[]{:S(2)}) collective-permute-start(bf16[1024,128]{1,0:T(8,128)(2,1)S(1)} %collective-permute-done.1.refs_2_), channel_id=1, source_target_pairs={{0,2},{2,0},{4,6},{6,4},{8,10},{10,8},{12,14},{14,12},{16,18},{18,... | collective-permute-start | bytes 786440 | tf_op jit(solution)/shard_map/ppermute | solution.py:48
  34.4 1.5 %collective-permute-start.6 = (bf16[1024,128]{1,0:T(8,128)(2,1)S(1)}, bf16[1024,128]{1,0:T(8,128)(2,1)S(1)}, u32[]{:S(2)}, u32[]{:S(2)}) collective-permute-start(bf16[1024,128]{1,0:T(8,128)(2,1)S(1)} %collective-permute-done.refs_1_), channel_id=1, source_target_pairs={{0,2},{2,0},{4,6},{6,4},{8,10},{10,8},{12,14},{14,12},{16,18},{18,... | collective-permute-start | bytes 786440 | tf_op jit(solution)/shard_map/ppermute | solution.py:48
  45.1 15.8 %all-to-all-start.1 = ((bf16[16,128,128]{2,1,0:T(8,128)(2,1)}), bf16[16,128,128]{2,1,0:T(8,128)(2,1)S(1)}, u32[]{:S(2)}, u32[]{:S(2)}) async-start(bf16[16,128,128]{2,1,0:T(8,128)(2,1)} %bitcast.4), calls=%async_computation.1 | async-start | bytes 1048576 | tf_op jit(solution)/shard_map/all_to_all | solution.py:52
  61.0 1.5 %copy-start.1 = (bf16[512,1792]{1,0:T(8,128)(2,1)S(1)}, bf16[512,1792]{1,0:T(8,128)(2,1)}, u32[]{:S(2)}) copy-start(bf16[512,1792]{1,0:T(8,128)(2,1)} %up_ref.1) | copy-start | bytes 5505028
  93.1 2.7 %collective-permute-start.7 = (bf16[4096,128]{1,0:T(8,128)(2,1)S(1)}, bf16[4096,128]{1,0:T(8,128)(2,1)S(1)}, u32[]{:S(2)}, u32[]{:S(2)}) collective-permute-start(bf16[4096,128]{1,0:T(8,128)(2,1)S(1)} %get-tuple-element.10), channel_id=1, source_target_pairs={{0,2},{2,0},{4,6},{6,4},{8,10},{10,8},{12,14},{14,12},{16,18},{18,... | collective-permute-start | bytes 3145736 | tf_op jit(solution)/shard_map/ppermute | solution.py:48
  96.0 9.3 %collective-permute-start.9 = (bf16[1024,128]{1,0:T(8,128)(2,1)S(1)}, bf16[1024,128]{1,0:T(8,128)(2,1)S(1)}, u32[]{:S(2)}, u32[]{:S(2)}) collective-permute-start(bf16[1024,128]{1,0:T(8,128)(2,1)S(1)} %get-tuple-element.16), channel_id=1, source_target_pairs={{0,13},{1,12},{2,6},{3,7},{4,0},{5,1},{6,10},{7,11},{8,4},{9,5},{1... | collective-permute-start | bytes 786440 | tf_op jit(solution)/shard_map/ppermute | solution.py:44
  99.3 9.8 %collective-permute-start.8 = (bf16[1024,128]{1,0:T(8,128)(2,1)S(1)}, bf16[1024,128]{1,0:T(8,128)(2,1)S(1)}, u32[]{:S(2)}, u32[]{:S(2)}) collective-permute-start(bf16[1024,128]{1,0:T(8,128)(2,1)S(1)} %get-tuple-element.15), channel_id=1, source_target_pairs={{0,4},{1,5},{2,15},{3,14},{4,8},{5,9},{6,2},{7,3},{8,12},{9,13},{1... | collective-permute-start | bytes 786440 | tf_op jit(solution)/shard_map/ppermute | solution.py:44
  105.4 7.7 %collective-permute-start.10 = (bf16[1024,128]{1,0:T(8,128)(2,1)S(1)}, bf16[1024,128]{1,0:T(8,128)(2,1)S(1)}, u32[]{:S(2)}, u32[]{:S(2)}) collective-permute-start(bf16[1024,128]{1,0:T(8,128)(2,1)S(1)} %add_convert_fusion.1), channel_id=1, source_target_pairs={{0,13},{1,12},{2,6},{3,7},{4,0},{5,1},{6,10},{7,11},{8,4},{9,5},{1... | collective-permute-start | bytes 786440 | tf_op jit(solution)/shard_map/ppermute | solution.py:44
  113.2 25.3 %copy-start.8 = (f32[13,64]{1,0:T(8,128)S(1)}, f32[13,64]{1,0:T(8,128)}, u32[]{:S(2)}) copy-start(f32[13,64]{1,0:T(8,128)} %param.19) | copy-start | bytes 9988
  113.2 25.9 %copy-start.6 = (bf16[13,64,128]{2,1,0:T(8,128)(2,1)S(1)}, bf16[13,64,128]{2,1,0:T(8,128)(2,1)}, u32[]{:S(2)}) copy-start(bf16[13,64,128]{2,1,0:T(8,128)(2,1)} %param.18) | copy-start | bytes 638980

commit v3 on v2

--- a/solution.py
+++ b/solution.py
@@ -66,20 +66,23 @@
 
 
 vmem = pl.BlockSpec(memory_space=pltpu.VMEM)
-smem = pl.BlockSpec(memory_space=pltpu.SMEM)
+anywhere = pl.BlockSpec(memory_space=pl.ANY)
 
 
 def lookup(ids, parts, samples, unroll=32):
     count = len(parts)
     places = GROUPS
 
-    def body(ids_ref, *refs):
-        part_refs, (out_ref, tab, acc) = refs[:count], refs[count:]
+    def body(ids_any, *refs):
+        part_refs, (out_ref, tab, acc, ids_ref, sem) = refs[:count], refs[count:]
+        copy = pltpu.make_async_copy(ids_any, ids_ref, sem)
+        copy.start()
         at = 0
         for ref in part_refs:
             tab[at : at + ref.shape[0], :] = ref[...].astype(f32)
             at += ref.shape[0]
         tab[at : at + 8, :] = jnp.zeros((8, EMB), f32)
+        copy.wait()
 
         def place(g, _):
             def some(i, _):
@@ -100,13 +103,15 @@
     return pl.pallas_call(
         body,
         out_shape=jax.ShapeDtypeStruct((places * samples, EMB), bf16),
-        in_specs=[smem] + [vmem] * count,
+        in_specs=[anywhere] + [vmem] * count,
         out_specs=vmem,
         scratch_shapes=[
             pltpu.VMEM((ROWS + 8, EMB), f32),
             pltpu.VMEM((places * samples, EMB), f32),
+            pltpu.SMEM((places * POOL * samples,), i32),
+            pltpu.SemaphoreType.DMA,
         ],
-        compiler_params=pltpu.CompilerParams(vmem_limit_bytes=24 << 20),
+        compiler_params=pltpu.CompilerParams(vmem_limit_bytes=10 << 20),
         name="lookup",
     )(ids, *parts)
 
@@ -115,11 +120,14 @@
     places, pair = GROUPS, 2
     totals = pair * POOL
 
-    def body(ids_ref, grads_ref, keep_ref, send_ref, *scratch):
-        accs, wide = scratch[:totals], scratch[totals]
+    def body(ids_any, grads_ref, keep_ref, send_ref, *scratch):
+        accs, (wide, ids_ref, sem) = scratch[:totals], scratch[totals:]
+        copy = pltpu.make_async_copy(ids_any, ids_ref, sem)
+        copy.start()
         for a in accs:
             a[...] = jnp.zeros((ROWS + 8, EMB), f32)
         wide[...] = grads_ref[...].astype(f32)
+        copy.wait()
 
         def place(g, _):
             def some(i, _):
@@ -165,11 +173,15 @@
             jax.ShapeDtypeStruct((HALF, EMB), f32),
             jax.ShapeDtypeStruct((HALF, EMB), bf16),
         ],
-        in_specs=[smem, vmem],
+        in_specs=[anywhere, vmem],
         out_specs=[vmem, vmem],
         scratch_shapes=[pltpu.VMEM((ROWS + 8, EMB), f32)] * totals
-        + [pltpu.VMEM((places * samples, EMB), f32)],
-        compiler_params=pltpu.CompilerParams(vmem_limit_bytes=44 << 20),
+        + [
+            pltpu.VMEM((places * samples, EMB), f32),
+            pltpu.SMEM((places * POOL * samples,), i32),
+            pltpu.SemaphoreType.DMA,
+        ],
+        compiler_params=pltpu.CompilerParams(vmem_limit_bytes=38 << 20),
         name="scatter",
     )(ids, grads)
 
@@ -177,20 +189,34 @@
 contract_last = (((1,), (1,)), ((), ()))
 
 
-def cross(dense, w1, w2, w3, pooled, down, up, bias, cot):
+def dot(a, b):
+    return jnp.dot(a, b, preferred_element_type=f32)
+
+
+def bottom(dense, w1, w2, w3):
+    def body(dense_ref, w1_ref, w2_ref, w3_ref, out_ref):
+        first = jax.nn.relu(dot(dense_ref[...], w1_ref[...])).astype(bf16)
+        second = jax.nn.relu(dot(first, w2_ref[...])).astype(bf16)
+        out_ref[...] = jax.nn.relu(dot(second, w3_ref[...])).astype(bf16)
+
+    return pl.pallas_call(
+        body,
+        out_shape=jax.ShapeDtypeStruct((dense.shape[0], EMB), bf16),
+        in_specs=[vmem] * 4,
+        out_specs=vmem,
+        compiler_params=pltpu.CompilerParams(vmem_limit_bytes=4 << 20),
+        name="bottom",
+    )(dense, w1, w2, w3)
+
+
+def cross(third, pooled, down, up, bias, cot):
     rows, width = cot.shape
     tables = width // EMB - 1
 
     def body(
-        dense_ref, w1_ref, w2_ref, w3_ref, pooled_ref, down_ref, up_ref, bias_ref, cot_ref,
-        crossed_ref, grad_ref, stacked,
+        third_ref, pooled_ref, down_ref, up_ref, bias_ref, cot_ref, crossed_ref, grad_ref, stacked
     ):
-        def dot(a, b):
-            return jnp.dot(a, b, preferred_element_type=f32)
-
-        first = jax.nn.relu(dot(dense_ref[...], w1_ref[...])).astype(bf16)
-        second = jax.nn.relu(dot(first, w2_ref[...])).astype(bf16)
-        stacked[:, :EMB] = jax.nn.relu(dot(second, w3_ref[...])).astype(bf16)
+        stacked[:, :EMB] = third_ref[...]
         for t in range(tables):
             stacked[:, (t + 1) * EMB : (t + 2) * EMB] = pooled_ref[t]
         low_rank = dot(stacked[...], down_ref[...]).astype(bf16)
@@ -219,12 +245,12 @@
             jax.ShapeDtypeStruct((rows, width), bf16),
             jax.ShapeDtypeStruct((GROUPS, rows, EMB), bf16),
         ],
-        in_specs=[vmem] * 9,
+        in_specs=[vmem] * 6,
         out_specs=[vmem, vmem],
         scratch_shapes=[pltpu.VMEM((rows, width), bf16)],
-        compiler_params=pltpu.CompilerParams(vmem_limit_bytes=20 << 20),
+        compiler_params=pltpu.CompilerParams(vmem_limit_bytes=6 << 20),
         name="cross",
-    )(dense, w1, w2, w3, pooled, down, up, bias.reshape(1, width), cot)
+    )(third, pooled, down, up, bias.reshape(1, width), cot)
 
 
 def per_device(
@@ -260,13 +286,17 @@
     high, low = got[:, ROWS_DEV : ROWS_DEV + pool], got[:, ROWS_DEV + pool :]
     at = (high.astype(f32) * 128.0 + low.astype(f32)).astype(i32).reshape(-1)
 
-    two = send_z(own, -2)
     one, three = send_z(own, -1), send_z(own, 1)
+    two = send_z(one, -1)
     pieces = [own, one, two, three] + [swap(x) for x in (own, three, two, one)]
     pooled = exchange(lookup(at, pieces, samples).reshape(GROUPS, samples, EMB))
 
     crossed, pooled_grad = cross(
-        dense_feats, bottom_w1, bottom_w2, bottom_w3, pooled, cross_down, cross_up, cross_bias,
+        bottom(dense_feats, bottom_w1, bottom_w2, bottom_w3),
+        pooled,
+        cross_down,
+        cross_up,
+        cross_bias,
         cotangent,
     )
     grads = exchange(pooled_grad).reshape(GROUPS * samples, EMB)

time: 142 us -> 138 us (0.972); the launches traced: 140 us -> 138 us
  blocking collectives: 54.1 us -> 52.1 us
    all_to_all x1, blocking collectives: 24.9 us -> 23.1 us  [exchange_reps(): lax.all_to_all(x, ('shard', 'rep'), split_axis=0, concat_axis=0, axis_ind...]
    ppermute x6, starting transfers between devices: 15.5 us -> 17.2 us  [send_z(): return lax.ppermute(x, ('shard', 'rep'), along_z(step))]
where the time goes in v3:
time: 138 us
  blocking collectives  52.1 us (38%)
  waiting for transfers between devices  32.1 us (23%)
  Pallas kernels  24.4 us (18%)
  starting transfers between devices  22.5 us (16%)
  other arithmetic  3.94 us (3%)
  local copies, waits for them, and re-layouts  1.84 us (1%)
    all_to_all x2, blocking collectives, exchange(): lax.all_to_all(x, 'shard', split_axis=0, concat_axis=0, axis_index_groups...  28.9 us
    all_to_all x1, blocking collectives, exchange_reps(): lax.all_to_all(x, ('shard', 'rep'), split_axis=0, concat_axis=0, axis_ind...  23.1 us
    ppermute x6, waiting for transfers between devices, send_z(): return lax.ppermute(x, ('shard', 'rep'), along_z(step))  17.7 us
    ppermute x6, starting transfers between devices, send_z(): return lax.ppermute(x, ('shard', 'rep'), along_z(step))  17.2 us
    pallas_call x1, Pallas kernels, scatter(): pl.pallas_call(body, out_shape=[jax.ShapeDtypeStruct((HALF, EMB), f32), j...  12.2 us
    all_to_all x1, waiting for transfers between devices, exchange(): lax.all_to_all(x, 'shard', split_axis=0, concat_axis=0, axis_index_groups...  10.2 us
    pallas_call x1, Pallas kernels, lookup(): pl.pallas_call(body, out_shape=jax.ShapeDtypeStruct((places * samples, EM...  8.94 us
    all_to_all x1, starting transfers between devices, exchange(): lax.all_to_all(x, 'shard', split_axis=0, concat_axis=0, axis_index_groups...  4.76 us
  transfers between devices with their start and end apart: 12, of which 8 were waited for; matrix products, arithmetic and copies ran while one was open for 0% of the time, Pallas kernels for 0%

profile of v3, /device:TPU:2, one launch (start us, length us, event | category | flops | bytes accessed | tf_op | source)
XLA Modules:
  0.0 137.7 jit_solution(8517460713641057330)
XLA Ops:
  0.7 0.8 broadcast_shift-right-arithmetic_fusion
  1.5 1.0 fusion.2
  2.5 14.9 %all_to_all.20 = bf16[16,72,128]{2,1,0:T(8,128)(2,1)S(1)} all-to-all(bf16[16,72,128]{2,1,0:T(8,128)(2,1)S(1)} %fusion.2), channel_id=1, replica_groups={{0,16,32,48,64,80,96,112,128,144,160,176,192,208,224,240},{2,18,34,50,6..., dimensions={0} | all-to-all | bytes 589824 | tf_op jit(solution)/shard_map/all_to_all | solution.py:52
  17.5 5.9 %collective-permute-start = (bf16[1024,128]{1,0:T(8,128)(2,1)S(1)}, bf16[1024,128]{1,0:T(8,128)(2,1)S(1)}, u32[]{:S(2)}, u32[]{:S(2)}) collective-permute-start(bf16[1024,128]{1,0:T(8,128)(2,1)S(1)} %bitcast.13), channel_id=1, source_target_pairs={{0,13},{1,12},{2,6},{3,7},{4,0},{5,1},{6,10},{7,11},{8,4},{9,5},{1... | collective-permute-start | bytes 786440 | tf_op jit(solution)/shard_map/ppermute | solution.py:44
  23.4 4.5 %collective-permute-done.refs_1_ = bf16[1024,128]{1,0:T(8,128)(2,1)S(1)} collective-permute-done((bf16[1024,128]{1,0:T(8,128)(2,1)S(1)}, bf16[1024,128]{1,0:T(8,128)(2,1)S(1)}, u32[]{:S(2)}, u32[]{:S(2)}) %collective-permute-start) | collective-permute-done | bytes 262176 | tf_op jit(solution)/shard_map/ppermute | solution.py:44
  27.9 3.7 %collective-permute-start.1 = (bf16[1024,128]{1,0:T(8,128)(2,1)S(1)}, bf16[1024,128]{1,0:T(8,128)(2,1)S(1)}, u32[]{:S(2)}, u32[]{:S(2)}) collective-permute-start(bf16[1024,128]{1,0:T(8,128)(2,1)S(1)} %collective-permute-done.refs_1_), channel_id=1, source_target_pairs={{0,13},{1,12},{2,6},{3,7},{4,0},{5,1},{6,10},{7,11},{8,4},{9,5},{1... | collective-permute-start | bytes 786440 | tf_op jit(solution)/shard_map/ppermute | solution.py:44
  31.6 0.5 collective-permute-start.6
  32.5 3.0 %collective-permute-done.1.refs_2_ = bf16[1024,128]{1,0:T(8,128)(2,1)S(1)} collective-permute-done((bf16[1024,128]{1,0:T(8,128)(2,1)S(1)}, bf16[1024,128]{1,0:T(8,128)(2,1)S(1)}, u32[]{:S(2)}, u32[]{:S(2)}) %collective-permute-start.1) | collective-permute-done | bytes 262176 | tf_op jit(solution)/shard_map/ppermute | solution.py:44
  35.6 1.5 %collective-permute-done.5.refs_6_ = bf16[1024,128]{1,0:T(8,128)(2,1)S(1)} collective-permute-done((bf16[1024,128]{1,0:T(8,128)(2,1)S(1)}, bf16[1024,128]{1,0:T(8,128)(2,1)S(1)}, u32[]{:S(2)}, u32[]{:S(2)}) %collective-permute-start.5) | collective-permute-done | bytes 262176 | tf_op jit(solution)/shard_map/ppermute | solution.py:48
  37.0 8.9 %lookup.1 = bf16[2048,128]{1,0:T(8,128)(2,1)} custom-call(s32[8192]{0:T(1024)S(1)} %bitcast.17, bf16[1024,128]{1,0:T(8,128)(2,1)S(1)} %bitcast.16, bf16[1024,128]{1,0:T(8,128)(2,1)S(1)} %collective-permute-done.refs_1_, bf16[1024,128]{1,0:T(8,128)(2,1)S(1)} %collective-permute-done.1.refs_2_, bf16[1024,128]{1,0:T(8,128)(2,1)S(1)} %collective-permute-done.2.refs_3_, ...), custom_call_target="tpu_custom_call" | custom-call | tf_op jit(solution)/shard_map/lookup/pallas_call | solution.py:103
  46.0 4.8 %all-to-all-start.1 = ((bf16[16,128,128]{2,1,0:T(8,128)(2,1)}), bf16[16,128,128]{2,1,0:T(8,128)(2,1)S(1)}, u32[]{:S(2)}, u32[]{:S(2)}) async-start(bf16[16,128,128]{2,1,0:T(8,128)(2,1)} %bitcast.4), calls=%async_computation.1 | async-start | bytes 1048576 | tf_op jit(solution)/shard_map/all_to_all | solution.py:52
  51.4 10.2 %all-to-all-done.1.pooled_ref = bf16[16,128,128]{2,1,0:T(8,128)(2,1)S(1)} async-done(((bf16[16,128,128]{2,1,0:T(8,128)(2,1)}), bf16[16,128,128]{2,1,0:T(8,128)(2,1)S(1)}, u32[]{:S(2)}, u32[]{:S(2)}) %all-to-all-start.1) | async-done | bytes 524320 | tf_op jit(solution)/shard_map/all_to_all | solution.py:52
  61.6 1.5 %copy-done.1 = bf16[512,1792]{1,0:T(8,128)(2,1)S(1)} copy-done((bf16[512,1792]{1,0:T(8,128)(2,1)S(1)}, bf16[512,1792]{1,0:T(8,128)(2,1)}, u32[]{:S(2)}) %copy-start.1) | copy-done | bytes 1835032
  63.1 2.7 %cross.1 = (bf16[128,1792]{1,0:T(8,128)(2,1)}, bf16[16,128,128]{2,1,0:T(8,128)(2,1)S(1)}) custom-call(bf16[128,128]{1,0:T(8,128)(2,1)S(1)} %bottom.1.third_ref, bf16[16,128,128]{2,1,0:T(8,128)(2,1)S(1)} %all-to-all-done.1.pooled_ref, bf16[1792,512]{1,0:T(8,128)(2,1)S(1)} %copy-done, bf16[512,1792]{1,0:T(8,128)(2,1)S(1)} %copy-done.1, ...), custom_call_target="tpu_custom_call" | custom-call | tf_op jit(solution)/shard_map/cross/pallas_call | solution.py:242
  65.8 14.0 %all_to_all.21 = bf16[16,128,128]{2,1,0:T(8,128)(2,1)S(1)} all-to-all(bf16[16,128,128]{2,1,0:T(8,128)(2,1)S(1)} %get-tuple-element.8), channel_id=1, replica_groups={{0,16,32,48,64,80,96,112,128,144,160,176,192,208,224,240},{2,18,34,50,6..., dimensions={0} | all-to-all | bytes 1048576 | tf_op jit(solution)/shard_map/all_to_all | solution.py:52
  79.8 12.2 %scatter.1 = (f32[4096,128]{1,0:T(8,128)S(1)}, bf16[4096,128]{1,0:T(8,128)(2,1)S(1)}) custom-call(s32[8192]{0:T(1024)S(1)} %bitcast.18, bf16[2048,128]{1,0:T(8,128)(2,1)S(1)} %bitcast.12), custom_call_target="tpu_custom_call" | custom-call | tf_op jit(solution)/shard_map/scatter/pallas_call | solution.py:170
  92.2 2.6 %collective-permute-done.7 = bf16[4096,128]{1,0:T(8,128)(2,1)S(1)} collective-permute-done((bf16[4096,128]{1,0:T(8,128)(2,1)S(1)}, bf16[4096,128]{1,0:T(8,128)(2,1)S(1)}, u32[]{:S(2)}, u32[]{:S(2)}) %collective-permute-start.7) | collective-permute-done | bytes 1048608 | tf_op jit(solution)/shard_map/ppermute | solution.py:48
  95.0 3.8 %collective-permute-start.9 = (bf16[1024,128]{1,0:T(8,128)(2,1)S(1)}, bf16[1024,128]{1,0:T(8,128)(2,1)S(1)}, u32[]{:S(2)}, u32[]{:S(2)}) collective-permute-start(bf16[1024,128]{1,0:T(8,128)(2,1)S(1)} %get-tuple-element.16), channel_id=1, source_target_pairs={{0,13},{1,12},{2,6},{3,7},{4,0},{5,1},{6,10},{7,11},{8,4},{9,5},{1... | collective-permute-start | bytes 786440 | tf_op jit(solution)/shard_map/ppermute | solution.py:44
  98.7 6.0 %collective-permute-done.9 = bf16[1024,128]{1,0:T(8,128)(2,1)S(1)} collective-permute-done((bf16[1024,128]{1,0:T(8,128)(2,1)S(1)}, bf16[1024,128]{1,0:T(8,128)(2,1)S(1)}, u32[]{:S(2)}, u32[]{:S(2)}) %collective-permute-start.9) | collective-permute-done | bytes 262176 | tf_op jit(solution)/shard_map/ppermute | solution.py:44
  104.8 3.8 %collective-permute-start.10 = (bf16[1024,128]{1,0:T(8,128)(2,1)S(1)}, bf16[1024,128]{1,0:T(8,128)(2,1)S(1)}, u32[]{:S(2)}, u32[]{:S(2)}) collective-permute-start(bf16[1024,128]{1,0:T(8,128)(2,1)S(1)} %add_convert_fusion.1), channel_id=1, source_target_pairs={{0,13},{1,12},{2,6},{3,7},{4,0},{5,1},{6,10},{7,11},{8,4},{9,5},{1... | collective-permute-start | bytes 786440 | tf_op jit(solution)/shard_map/ppermute | solution.py:44
  108.6 3.9 %collective-permute-done.10 = bf16[1024,128]{1,0:T(8,128)(2,1)S(1)} collective-permute-done((bf16[1024,128]{1,0:T(8,128)(2,1)S(1)}, bf16[1024,128]{1,0:T(8,128)(2,1)S(1)}, u32[]{:S(2)}, u32[]{:S(2)}) %collective-permute-start.10) | collective-permute-done | bytes 262176 | tf_op jit(solution)/shard_map/ppermute | solution.py:44
  112.7 23.1 %all_to_all.22 = bf16[32,64,128]{2,1,0:T(8,128)(2,1)S(1)} all-to-all(bf16[32,64,128]{2,1,0:T(8,128)(2,1)S(1)} %bitcast.19), channel_id=1, replica_groups={{0,1,16,17,32,33,48,49,64,65,80,81,96,97,112,113,128,129,144,145,160,16..., dimensions={0} | all-to-all | bytes 1048576 | tf_op jit(solution)/shard_map/all_to_all | solution.py:58
  136.2 0.6 sqrt_add_fusion
  136.8 0.9 divide_subtract_fusion
  (44 shorter events, 1.9 us)
Async XLA Ops:
  17.4 33.4 %copy-start.7 = (f32[1792]{0:T(1024)S(1)}, f32[1792]{0:T(1024)}, u32[]{:S(2)}) copy-start(f32[1792]{0:T(1024)} %param.22) | copy-start | bytes 21508
  17.4 33.4 %copy-start.9 = (bf16[128,13]{0,1:T(8,128)(2,1)S(1)}, bf16[128,13]{0,1:T(8,128)(2,1)}, u32[]{:S(2)}) copy-start(bf16[128,13]{0,1:T(8,128)(2,1)} %param.12) | copy-start | bytes 9988
  17.4 33.5 %copy-start.3 = (bf16[512,256]{1,0:T(8,128)(2,1)S(1)}, bf16[512,256]{1,0:T(8,128)(2,1)}, u32[]{:S(2)}) copy-start(bf16[512,256]{1,0:T(8,128)(2,1)} %w2_ref.1) | copy-start | bytes 786436
  17.4 33.5 %copy-start.4 = (bf16[256,128]{1,0:T(8,128)(2,1)S(1)}, bf16[256,128]{1,0:T(8,128)(2,1)}, u32[]{:S(2)}) copy-start(bf16[256,128]{1,0:T(8,128)(2,1)} %w3_ref.1) | copy-start | bytes 196612
  17.4 33.5 %copy-start.5 = (bf16[13,512]{1,0:T(8,128)(2,1)S(1)}, bf16[13,512]{1,0:T(8,128)(2,1)}, u32[]{:S(2)}) copy-start(bf16[13,512]{1,0:T(8,128)(2,1)} %w1_ref.1) | copy-start | bytes 39940
  17.5 10.5 %collective-permute-start = (bf16[1024,128]{1,0:T(8,128)(2,1)S(1)}, bf16[1024,128]{1,0:T(8,128)(2,1)S(1)}, u32[]{:S(2)}, u32[]{:S(2)}) collective-permute-start(bf16[1024,128]{1,0:T(8,128)(2,1)S(1)} %bitcast.13), channel_id=1, source_target_pairs={{0,13},{1,12},{2,6},{3,7},{4,0},{5,1},{6,10},{7,11},{8,4},{9,5},{1... | collective-permute-start | bytes 786440 | tf_op jit(solution)/shard_map/ppermute | solution.py:44
  23.4 9.1 %collective-permute-start.2 = (bf16[1024,128]{1,0:T(8,128)(2,1)S(1)}, bf16[1024,128]{1,0:T(8,128)(2,1)S(1)}, u32[]{:S(2)}, u32[]{:S(2)}) collective-permute-start(bf16[1024,128]{1,0:T(8,128)(2,1)S(1)} %bitcast.14), channel_id=1, source_target_pairs={{0,4},{1,5},{2,15},{3,14},{4,8},{5,9},{6,2},{7,3},{8,12},{9,13},{1... | collective-permute-start | bytes 786440 | tf_op jit(solution)/shard_map/ppermute | solution.py:44
  27.9 7.6 %collective-permute-start.1 = (bf16[1024,128]{1,0:T(8,128)(2,1)S(1)}, bf16[1024,128]{1,0:T(8,128)(2,1)S(1)}, u32[]{:S(2)}, u32[]{:S(2)}) collective-permute-start(bf16[1024,128]{1,0:T(8,128)(2,1)S(1)} %collective-permute-done.refs_1_), channel_id=1, source_target_pairs={{0,13},{1,12},{2,6},{3,7},{4,0},{5,1},{6,10},{7,11},{8,4},{9,5},{1... | collective-permute-start | bytes 786440 | tf_op jit(solution)/shard_map/ppermute | solution.py:44
  31.6 3.9 %collective-permute-start.3 = (bf16[1024,128]{1,0:T(8,128)(2,1)S(1)}, bf16[1024,128]{1,0:T(8,128)(2,1)S(1)}, u32[]{:S(2)}, u32[]{:S(2)}) collective-permute-start(bf16[1024,128]{1,0:T(8,128)(2,1)S(1)} %bitcast.15), channel_id=1, source_target_pairs={{0,2},{2,0},{4,6},{6,4},{8,10},{10,8},{12,14},{14,12},{16,18},{18,... | collective-permute-start | bytes 786440 | tf_op jit(solution)/shard_map/ppermute | solution.py:48
  31.6 4.0 %collective-permute-start.6 = (bf16[1024,128]{1,0:T(8,128)(2,1)S(1)}, bf16[1024,128]{1,0:T(8,128)(2,1)S(1)}, u32[]{:S(2)}, u32[]{:S(2)}) collective-permute-start(bf16[1024,128]{1,0:T(8,128)(2,1)S(1)} %collective-permute-done.refs_1_), channel_id=1, source_target_pairs={{0,2},{2,0},{4,6},{6,4},{8,10},{10,8},{12,14},{14,12},{16,18},{18,... | collective-permute-start | bytes 786440 | tf_op jit(solution)/shard_map/ppermute | solution.py:48
  32.5 3.0 %collective-permute-start.4 = (bf16[1024,128]{1,0:T(8,128)(2,1)S(1)}, bf16[1024,128]{1,0:T(8,128)(2,1)S(1)}, u32[]{:S(2)}, u32[]{:S(2)}) collective-permute-start(bf16[1024,128]{1,0:T(8,128)(2,1)S(1)} %collective-permute-done.2.refs_3_), channel_id=1, source_target_pairs={{0,2},{2,0},{4,6},{6,4},{8,10},{10,8},{12,14},{14,12},{16,18},{18,... | collective-permute-start | bytes 786440 | tf_op jit(solution)/shard_map/ppermute | solution.py:48
  35.5 1.5 %collective-permute-start.5 = (bf16[1024,128]{1,0:T(8,128)(2,1)S(1)}, bf16[1024,128]{1,0:T(8,128)(2,1)S(1)}, u32[]{:S(2)}, u32[]{:S(2)}) collective-permute-start(bf16[1024,128]{1,0:T(8,128)(2,1)S(1)} %collective-permute-done.1.refs_2_), channel_id=1, source_target_pairs={{0,2},{2,0},{4,6},{6,4},{8,10},{10,8},{12,14},{14,12},{16,18},{18,... | collective-permute-start | bytes 786440 | tf_op jit(solution)/shard_map/ppermute | solution.py:48
  35.5 26.1 %copy-start = (bf16[1792,512]{1,0:T(8,128)(2,1)S(1)}, bf16[1792,512]{1,0:T(8,128)(2,1)}, u32[]{:S(2)}) copy-start(bf16[1792,512]{1,0:T(8,128)(2,1)} %down_ref.1) | copy-start | bytes 5505028
  35.5 26.1 %copy-start.2 = (bf16[128,1792]{1,0:T(8,128)(2,1)S(1)}, bf16[128,1792]{1,0:T(8,128)(2,1)}, u32[]{:S(2)}) copy-start(bf16[128,1792]{1,0:T(8,128)(2,1)} %cot_ref.1) | copy-start | bytes 1376260
  46.0 15.6 %all-to-all-start.1 = ((bf16[16,128,128]{2,1,0:T(8,128)(2,1)}), bf16[16,128,128]{2,1,0:T(8,128)(2,1)S(1)}, u32[]{:S(2)}, u32[]{:S(2)}) async-start(bf16[16,128,128]{2,1,0:T(8,128)(2,1)} %bitcast.4), calls=%async_computation.1 | async-start | bytes 1048576 | tf_op jit(solution)/shard_map/all_to_all | solution.py:52
  61.6 1.5 %copy-start.1 = (bf16[512,1792]{1,0:T(8,128)(2,1)S(1)}, bf16[512,1792]{1,0:T(8,128)(2,1)}, u32[]{:S(2)}) copy-start(bf16[512,1792]{1,0:T(8,128)(2,1)} %up_ref.1) | copy-start | bytes 5505028
  92.1 2.7 %collective-permute-start.7 = (bf16[4096,128]{1,0:T(8,128)(2,1)S(1)}, bf16[4096,128]{1,0:T(8,128)(2,1)S(1)}, u32[]{:S(2)}, u32[]{:S(2)}) collective-permute-start(bf16[4096,128]{1,0:T(8,128)(2,1)S(1)} %get-tuple-element.10), channel_id=1, source_target_pairs={{0,2},{2,0},{4,6},{6,4},{8,10},{10,8},{12,14},{14,12},{16,18},{18,... | collective-permute-start | bytes 3145736 | tf_op jit(solution)/shard_map/ppermute | solution.py:48
  95.0 9.7 %collective-permute-start.9 = (bf16[1024,128]{1,0:T(8,128)(2,1)S(1)}, bf16[1024,128]{1,0:T(8,128)(2,1)S(1)}, u32[]{:S(2)}, u32[]{:S(2)}) collective-permute-start(bf16[1024,128]{1,0:T(8,128)(2,1)S(1)} %get-tuple-element.16), channel_id=1, source_target_pairs={{0,13},{1,12},{2,6},{3,7},{4,0},{5,1},{6,10},{7,11},{8,4},{9,5},{1... | collective-permute-start | bytes 786440 | tf_op jit(solution)/shard_map/ppermute | solution.py:44
  98.7 9.8 %collective-permute-start.8 = (bf16[1024,128]{1,0:T(8,128)(2,1)S(1)}, bf16[1024,128]{1,0:T(8,128)(2,1)S(1)}, u32[]{:S(2)}, u32[]{:S(2)}) collective-permute-start(bf16[1024,128]{1,0:T(8,128)(2,1)S(1)} %get-tuple-element.15), channel_id=1, source_target_pairs={{0,4},{1,5},{2,15},{3,14},{4,8},{5,9},{6,2},{7,3},{8,12},{9,13},{1... | collective-permute-start | bytes 786440 | tf_op jit(solution)/shard_map/ppermute | solution.py:44
  104.8 7.7 %collective-permute-start.10 = (bf16[1024,128]{1,0:T(8,128)(2,1)S(1)}, bf16[1024,128]{1,0:T(8,128)(2,1)S(1)}, u32[]{:S(2)}, u32[]{:S(2)}) collective-permute-start(bf16[1024,128]{1,0:T(8,128)(2,1)S(1)} %add_convert_fusion.1), channel_id=1, source_target_pairs={{0,13},{1,12},{2,6},{3,7},{4,0},{5,1},{6,10},{7,11},{8,4},{9,5},{1... | collective-permute-start | bytes 786440 | tf_op jit(solution)/shard_map/ppermute | solution.py:44
  112.6 23.6 %copy-start.8 = (f32[13,64]{1,0:T(8,128)S(1)}, f32[13,64]{1,0:T(8,128)}, u32[]{:S(2)}) copy-start(f32[13,64]{1,0:T(8,128)} %param.19) | copy-start | bytes 9988
  112.6 24.2 %copy-start.6 = (bf16[13,64,128]{2,1,0:T(8,128)(2,1)S(1)}, bf16[13,64,128]{2,1,0:T(8,128)(2,1)}, u32[]{:S(2)}) copy-start(bf16[13,64,128]{2,1,0:T(8,128)(2,1)} %param.18) | copy-start | bytes 638980

commit v4 on v3

--- a/solution.py
+++ b/solution.py
@@ -69,7 +69,7 @@
 anywhere = pl.BlockSpec(memory_space=pl.ANY)
 
 
-def lookup(ids, parts, samples, unroll=32):
+def lookup(ids, parts, samples, unroll=128):
     count = len(parts)
     places = GROUPS
 
@@ -116,7 +116,7 @@
     )(ids, *parts)
 
 
-def scatter(ids, grads, samples, unroll=16):
+def scatter(ids, grads, samples, unroll=64):
     places, pair = GROUPS, 2
     totals = pair * POOL
 

time: 138 us -> 137 us (level)
  no operation moved by 1% of the time
where the time goes in v4:
time: 137 us
  blocking collectives  52.1 us (38%)
  waiting for transfers between devices  32.1 us (23%)
  Pallas kernels  23.6 us (17%)
  starting transfers between devices  22.7 us (17%)
  other arithmetic  3.94 us (3%)
  local copies, waits for them, and re-layouts  1.84 us (1%)
    all_to_all x2, blocking collectives, exchange(): lax.all_to_all(x, 'shard', split_axis=0, concat_axis=0, axis_index_groups...  28.9 us
    all_to_all x1, blocking collectives, exchange_reps(): lax.all_to_all(x, ('shard', 'rep'), split_axis=0, concat_axis=0, axis_ind...  23.2 us
    ppermute x6, waiting for transfers between devices, send_z(): return lax.ppermute(x, ('shard', 'rep'), along_z(step))  17.7 us
    ppermute x6, starting transfers between devices, send_z(): return lax.ppermute(x, ('shard', 'rep'), along_z(step))  17.3 us
    pallas_call x1, Pallas kernels, scatter(): pl.pallas_call(body, out_shape=[jax.ShapeDtypeStruct((HALF, EMB), f32), j...  11.9 us
    all_to_all x1, waiting for transfers between devices, exchange(): lax.all_to_all(x, 'shard', split_axis=0, concat_axis=0, axis_index_groups...  10.2 us
    pallas_call x1, Pallas kernels, lookup(): pl.pallas_call(body, out_shape=jax.ShapeDtypeStruct((places * samples, EM...  8.51 us
    all_to_all x1, starting transfers between devices, exchange(): lax.all_to_all(x, 'shard', split_axis=0, concat_axis=0, axis_index_groups...  4.76 us
  transfers between devices with their start and end apart: 12, of which 8 were waited for; matrix products, arithmetic and copies ran while one was open for 0% of the time, Pallas kernels for 0%

profile of v4, /device:TPU:2, one launch (start us, length us, event | category | flops | bytes accessed | tf_op | source)
XLA Modules:
  0.0 137.1 jit_solution(9052550329544675307)
XLA Ops:
  0.7 0.8 broadcast_shift-right-arithmetic_fusion
  1.5 1.0 fusion.2
  2.5 14.9 %all_to_all.20 = bf16[16,72,128]{2,1,0:T(8,128)(2,1)S(1)} all-to-all(bf16[16,72,128]{2,1,0:T(8,128)(2,1)S(1)} %fusion.2), channel_id=1, replica_groups={{0,16,32,48,64,80,96,112,128,144,160,176,192,208,224,240},{2,18,34,50,6..., dimensions={0} | all-to-all | bytes 589824 | tf_op jit(solution)/shard_map/all_to_all | solution.py:52
  17.5 5.9 %collective-permute-start = (bf16[1024,128]{1,0:T(8,128)(2,1)S(1)}, bf16[1024,128]{1,0:T(8,128)(2,1)S(1)}, u32[]{:S(2)}, u32[]{:S(2)}) collective-permute-start(bf16[1024,128]{1,0:T(8,128)(2,1)S(1)} %bitcast.13), channel_id=1, source_target_pairs={{0,13},{1,12},{2,6},{3,7},{4,0},{5,1},{6,10},{7,11},{8,4},{9,5},{1... | collective-permute-start | bytes 786440 | tf_op jit(solution)/shard_map/ppermute | solution.py:44
  23.4 4.5 %collective-permute-done.refs_1_ = bf16[1024,128]{1,0:T(8,128)(2,1)S(1)} collective-permute-done((bf16[1024,128]{1,0:T(8,128)(2,1)S(1)}, bf16[1024,128]{1,0:T(8,128)(2,1)S(1)}, u32[]{:S(2)}, u32[]{:S(2)}) %collective-permute-start) | collective-permute-done | bytes 262176 | tf_op jit(solution)/shard_map/ppermute | solution.py:44
  27.9 3.7 %collective-permute-start.1 = (bf16[1024,128]{1,0:T(8,128)(2,1)S(1)}, bf16[1024,128]{1,0:T(8,128)(2,1)S(1)}, u32[]{:S(2)}, u32[]{:S(2)}) collective-permute-start(bf16[1024,128]{1,0:T(8,128)(2,1)S(1)} %collective-permute-done.refs_1_), channel_id=1, source_target_pairs={{0,13},{1,12},{2,6},{3,7},{4,0},{5,1},{6,10},{7,11},{8,4},{9,5},{1... | collective-permute-start | bytes 786440 | tf_op jit(solution)/shard_map/ppermute | solution.py:44
  31.6 0.5 collective-permute-start.6
  32.5 3.0 %collective-permute-done.1.refs_2_ = bf16[1024,128]{1,0:T(8,128)(2,1)S(1)} collective-permute-done((bf16[1024,128]{1,0:T(8,128)(2,1)S(1)}, bf16[1024,128]{1,0:T(8,128)(2,1)S(1)}, u32[]{:S(2)}, u32[]{:S(2)}) %collective-permute-start.1) | collective-permute-done | bytes 262176 | tf_op jit(solution)/shard_map/ppermute | solution.py:44
  35.6 1.5 %collective-permute-done.5.refs_6_ = bf16[1024,128]{1,0:T(8,128)(2,1)S(1)} collective-permute-done((bf16[1024,128]{1,0:T(8,128)(2,1)S(1)}, bf16[1024,128]{1,0:T(8,128)(2,1)S(1)}, u32[]{:S(2)}, u32[]{:S(2)}) %collective-permute-start.5) | collective-permute-done | bytes 262176 | tf_op jit(solution)/shard_map/ppermute | solution.py:48
  37.0 8.5 %lookup.1 = bf16[2048,128]{1,0:T(8,128)(2,1)} custom-call(s32[8192]{0:T(1024)S(1)} %bitcast.17, bf16[1024,128]{1,0:T(8,128)(2,1)S(1)} %bitcast.16, bf16[1024,128]{1,0:T(8,128)(2,1)S(1)} %collective-permute-done.refs_1_, bf16[1024,128]{1,0:T(8,128)(2,1)S(1)} %collective-permute-done.1.refs_2_, bf16[1024,128]{1,0:T(8,128)(2,1)S(1)} %collective-permute-done.2.refs_3_, ...), custom_call_target="tpu_custom_call" | custom-call | tf_op jit(solution)/shard_map/lookup/pallas_call | solution.py:103
  45.6 4.8 %all-to-all-start.1 = ((bf16[16,128,128]{2,1,0:T(8,128)(2,1)}), bf16[16,128,128]{2,1,0:T(8,128)(2,1)S(1)}, u32[]{:S(2)}, u32[]{:S(2)}) async-start(bf16[16,128,128]{2,1,0:T(8,128)(2,1)} %bitcast.4), calls=%async_computation.1 | async-start | bytes 1048576 | tf_op jit(solution)/shard_map/all_to_all | solution.py:52
  51.0 10.2 %all-to-all-done.1.pooled_ref = bf16[16,128,128]{2,1,0:T(8,128)(2,1)S(1)} async-done(((bf16[16,128,128]{2,1,0:T(8,128)(2,1)}), bf16[16,128,128]{2,1,0:T(8,128)(2,1)S(1)}, u32[]{:S(2)}, u32[]{:S(2)}) %all-to-all-start.1) | async-done | bytes 524320 | tf_op jit(solution)/shard_map/all_to_all | solution.py:52
  61.2 1.5 %copy-done.1 = bf16[512,1792]{1,0:T(8,128)(2,1)S(1)} copy-done((bf16[512,1792]{1,0:T(8,128)(2,1)S(1)}, bf16[512,1792]{1,0:T(8,128)(2,1)}, u32[]{:S(2)}) %copy-start.1) | copy-done | bytes 1835032
  62.7 2.7 %cross.1 = (bf16[128,1792]{1,0:T(8,128)(2,1)}, bf16[16,128,128]{2,1,0:T(8,128)(2,1)S(1)}) custom-call(bf16[128,128]{1,0:T(8,128)(2,1)S(1)} %bottom.1.third_ref, bf16[16,128,128]{2,1,0:T(8,128)(2,1)S(1)} %all-to-all-done.1.pooled_ref, bf16[1792,512]{1,0:T(8,128)(2,1)S(1)} %copy-done, bf16[512,1792]{1,0:T(8,128)(2,1)S(1)} %copy-done.1, ...), custom_call_target="tpu_custom_call" | custom-call | tf_op jit(solution)/shard_map/cross/pallas_call | solution.py:242
  65.4 14.0 %all_to_all.21 = bf16[16,128,128]{2,1,0:T(8,128)(2,1)S(1)} all-to-all(bf16[16,128,128]{2,1,0:T(8,128)(2,1)S(1)} %get-tuple-element.8), channel_id=1, replica_groups={{0,16,32,48,64,80,96,112,128,144,160,176,192,208,224,240},{2,18,34,50,6..., dimensions={0} | all-to-all | bytes 1048576 | tf_op jit(solution)/shard_map/all_to_all | solution.py:52
  79.4 11.9 %scatter.1 = (f32[4096,128]{1,0:T(8,128)S(1)}, bf16[4096,128]{1,0:T(8,128)(2,1)S(1)}) custom-call(s32[8192]{0:T(1024)S(1)} %bitcast.18, bf16[2048,128]{1,0:T(8,128)(2,1)S(1)} %bitcast.12), custom_call_target="tpu_custom_call" | custom-call | tf_op jit(solution)/shard_map/scatter/pallas_call | solution.py:170
  91.4 2.6 %collective-permute-done.7 = bf16[4096,128]{1,0:T(8,128)(2,1)S(1)} collective-permute-done((bf16[4096,128]{1,0:T(8,128)(2,1)S(1)}, bf16[4096,128]{1,0:T(8,128)(2,1)S(1)}, u32[]{:S(2)}, u32[]{:S(2)}) %collective-permute-start.7) | collective-permute-done | bytes 1048608 | tf_op jit(solution)/shard_map/ppermute | solution.py:48
  94.1 3.9 %collective-permute-start.9 = (bf16[1024,128]{1,0:T(8,128)(2,1)S(1)}, bf16[1024,128]{1,0:T(8,128)(2,1)S(1)}, u32[]{:S(2)}, u32[]{:S(2)}) collective-permute-start(bf16[1024,128]{1,0:T(8,128)(2,1)S(1)} %get-tuple-element.16), channel_id=1, source_target_pairs={{0,13},{1,12},{2,6},{3,7},{4,0},{5,1},{6,10},{7,11},{8,4},{9,5},{1... | collective-permute-start | bytes 786440 | tf_op jit(solution)/shard_map/ppermute | solution.py:44
  98.1 6.0 %collective-permute-done.9 = bf16[1024,128]{1,0:T(8,128)(2,1)S(1)} collective-permute-done((bf16[1024,128]{1,0:T(8,128)(2,1)S(1)}, bf16[1024,128]{1,0:T(8,128)(2,1)S(1)}, u32[]{:S(2)}, u32[]{:S(2)}) %collective-permute-start.9) | collective-permute-done | bytes 262176 | tf_op jit(solution)/shard_map/ppermute | solution.py:44
  104.1 3.8 %collective-permute-start.10 = (bf16[1024,128]{1,0:T(8,128)(2,1)S(1)}, bf16[1024,128]{1,0:T(8,128)(2,1)S(1)}, u32[]{:S(2)}, u32[]{:S(2)}) collective-permute-start(bf16[1024,128]{1,0:T(8,128)(2,1)S(1)} %add_convert_fusion.1), channel_id=1, source_target_pairs={{0,13},{1,12},{2,6},{3,7},{4,0},{5,1},{6,10},{7,11},{8,4},{9,5},{1... | collective-permute-start | bytes 786440 | tf_op jit(solution)/shard_map/ppermute | solution.py:44
  107.9 3.9 %collective-permute-done.10 = bf16[1024,128]{1,0:T(8,128)(2,1)S(1)} collective-permute-done((bf16[1024,128]{1,0:T(8,128)(2,1)S(1)}, bf16[1024,128]{1,0:T(8,128)(2,1)S(1)}, u32[]{:S(2)}, u32[]{:S(2)}) %collective-permute-start.10) | collective-permute-done | bytes 262176 | tf_op jit(solution)/shard_map/ppermute | solution.py:44
  112.0 23.2 %all_to_all.22 = bf16[32,64,128]{2,1,0:T(8,128)(2,1)S(1)} all-to-all(bf16[32,64,128]{2,1,0:T(8,128)(2,1)S(1)} %bitcast.19), channel_id=1, replica_groups={{0,1,16,17,32,33,48,49,64,65,80,81,96,97,112,113,128,129,144,145,160,16..., dimensions={0} | all-to-all | bytes 1048576 | tf_op jit(solution)/shard_map/all_to_all | solution.py:58
  135.5 0.6 sqrt_add_fusion
  136.1 0.9 divide_subtract_fusion
  (44 shorter events, 1.9 us)
Async XLA Ops:
  17.4 32.9 %copy-start.7 = (f32[1792]{0:T(1024)S(1)}, f32[1792]{0:T(1024)}, u32[]{:S(2)}) copy-start(f32[1792]{0:T(1024)} %param.22) | copy-start | bytes 21508
  17.4 32.9 %copy-start.9 = (bf16[128,13]{0,1:T(8,128)(2,1)S(1)}, bf16[128,13]{0,1:T(8,128)(2,1)}, u32[]{:S(2)}) copy-start(bf16[128,13]{0,1:T(8,128)(2,1)} %param.12) | copy-start | bytes 9988
  17.4 33.1 %copy-start.3 = (bf16[512,256]{1,0:T(8,128)(2,1)S(1)}, bf16[512,256]{1,0:T(8,128)(2,1)}, u32[]{:S(2)}) copy-start(bf16[512,256]{1,0:T(8,128)(2,1)} %w2_ref.1) | copy-start | bytes 786436
  17.4 33.1 %copy-start.4 = (bf16[256,128]{1,0:T(8,128)(2,1)S(1)}, bf16[256,128]{1,0:T(8,128)(2,1)}, u32[]{:S(2)}) copy-start(bf16[256,128]{1,0:T(8,128)(2,1)} %w3_ref.1) | copy-start | bytes 196612
  17.4 33.1 %copy-start.5 = (bf16[13,512]{1,0:T(8,128)(2,1)S(1)}, bf16[13,512]{1,0:T(8,128)(2,1)}, u32[]{:S(2)}) copy-start(bf16[13,512]{1,0:T(8,128)(2,1)} %w1_ref.1) | copy-start | bytes 39940
  17.5 10.5 %collective-permute-start = (bf16[1024,128]{1,0:T(8,128)(2,1)S(1)}, bf16[1024,128]{1,0:T(8,128)(2,1)S(1)}, u32[]{:S(2)}, u32[]{:S(2)}) collective-permute-start(bf16[1024,128]{1,0:T(8,128)(2,1)S(1)} %bitcast.13), channel_id=1, source_target_pairs={{0,13},{1,12},{2,6},{3,7},{4,0},{5,1},{6,10},{7,11},{8,4},{9,5},{1... | collective-permute-start | bytes 786440 | tf_op jit(solution)/shard_map/ppermute | solution.py:44
  23.4 9.1 %collective-permute-start.2 = (bf16[1024,128]{1,0:T(8,128)(2,1)S(1)}, bf16[1024,128]{1,0:T(8,128)(2,1)S(1)}, u32[]{:S(2)}, u32[]{:S(2)}) collective-permute-start(bf16[1024,128]{1,0:T(8,128)(2,1)S(1)} %bitcast.14), channel_id=1, source_target_pairs={{0,4},{1,5},{2,15},{3,14},{4,8},{5,9},{6,2},{7,3},{8,12},{9,13},{1... | collective-permute-start | bytes 786440 | tf_op jit(solution)/shard_map/ppermute | solution.py:44
  27.9 7.6 %collective-permute-start.1 = (bf16[1024,128]{1,0:T(8,128)(2,1)S(1)}, bf16[1024,128]{1,0:T(8,128)(2,1)S(1)}, u32[]{:S(2)}, u32[]{:S(2)}) collective-permute-start(bf16[1024,128]{1,0:T(8,128)(2,1)S(1)} %collective-permute-done.refs_1_), channel_id=1, source_target_pairs={{0,13},{1,12},{2,6},{3,7},{4,0},{5,1},{6,10},{7,11},{8,4},{9,5},{1... | collective-permute-start | bytes 786440 | tf_op jit(solution)/shard_map/ppermute | solution.py:44
  31.6 3.9 %collective-permute-start.3 = (bf16[1024,128]{1,0:T(8,128)(2,1)S(1)}, bf16[1024,128]{1,0:T(8,128)(2,1)S(1)}, u32[]{:S(2)}, u32[]{:S(2)}) collective-permute-start(bf16[1024,128]{1,0:T(8,128)(2,1)S(1)} %bitcast.15), channel_id=1, source_target_pairs={{0,2},{2,0},{4,6},{6,4},{8,10},{10,8},{12,14},{14,12},{16,18},{18,... | collective-permute-start | bytes 786440 | tf_op jit(solution)/shard_map/ppermute | solution.py:48
  31.6 4.0 %collective-permute-start.6 = (bf16[1024,128]{1,0:T(8,128)(2,1)S(1)}, bf16[1024,128]{1,0:T(8,128)(2,1)S(1)}, u32[]{:S(2)}, u32[]{:S(2)}) collective-permute-start(bf16[1024,128]{1,0:T(8,128)(2,1)S(1)} %collective-permute-done.refs_1_), channel_id=1, source_target_pairs={{0,2},{2,0},{4,6},{6,4},{8,10},{10,8},{12,14},{14,12},{16,18},{18,... | collective-permute-start | bytes 786440 | tf_op jit(solution)/shard_map/ppermute | solution.py:48
  32.5 3.0 %collective-permute-start.4 = (bf16[1024,128]{1,0:T(8,128)(2,1)S(1)}, bf16[1024,128]{1,0:T(8,128)(2,1)S(1)}, u32[]{:S(2)}, u32[]{:S(2)}) collective-permute-start(bf16[1024,128]{1,0:T(8,128)(2,1)S(1)} %collective-permute-done.2.refs_3_), channel_id=1, source_target_pairs={{0,2},{2,0},{4,6},{6,4},{8,10},{10,8},{12,14},{14,12},{16,18},{18,... | collective-permute-start | bytes 786440 | tf_op jit(solution)/shard_map/ppermute | solution.py:48
  35.5 1.5 %collective-permute-start.5 = (bf16[1024,128]{1,0:T(8,128)(2,1)S(1)}, bf16[1024,128]{1,0:T(8,128)(2,1)S(1)}, u32[]{:S(2)}, u32[]{:S(2)}) collective-permute-start(bf16[1024,128]{1,0:T(8,128)(2,1)S(1)} %collective-permute-done.1.refs_2_), channel_id=1, source_target_pairs={{0,2},{2,0},{4,6},{6,4},{8,10},{10,8},{12,14},{14,12},{16,18},{18,... | collective-permute-start | bytes 786440 | tf_op jit(solution)/shard_map/ppermute | solution.py:48
  35.5 25.6 %copy-start = (bf16[1792,512]{1,0:T(8,128)(2,1)S(1)}, bf16[1792,512]{1,0:T(8,128)(2,1)}, u32[]{:S(2)}) copy-start(bf16[1792,512]{1,0:T(8,128)(2,1)} %down_ref.1) | copy-start | bytes 5505028
  35.5 25.6 %copy-start.2 = (bf16[128,1792]{1,0:T(8,128)(2,1)S(1)}, bf16[128,1792]{1,0:T(8,128)(2,1)}, u32[]{:S(2)}) copy-start(bf16[128,1792]{1,0:T(8,128)(2,1)} %cot_ref.1) | copy-start | bytes 1376260
  45.6 15.6 %all-to-all-start.1 = ((bf16[16,128,128]{2,1,0:T(8,128)(2,1)}), bf16[16,128,128]{2,1,0:T(8,128)(2,1)S(1)}, u32[]{:S(2)}, u32[]{:S(2)}) async-start(bf16[16,128,128]{2,1,0:T(8,128)(2,1)} %bitcast.4), calls=%async_computation.1 | async-start | bytes 1048576 | tf_op jit(solution)/shard_map/all_to_all | solution.py:52
  61.2 1.5 %copy-start.1 = (bf16[512,1792]{1,0:T(8,128)(2,1)S(1)}, bf16[512,1792]{1,0:T(8,128)(2,1)}, u32[]{:S(2)}) copy-start(bf16[512,1792]{1,0:T(8,128)(2,1)} %up_ref.1) | copy-start | bytes 5505028
  91.3 2.7 %collective-permute-start.7 = (bf16[4096,128]{1,0:T(8,128)(2,1)S(1)}, bf16[4096,128]{1,0:T(8,128)(2,1)S(1)}, u32[]{:S(2)}, u32[]{:S(2)}) collective-permute-start(bf16[4096,128]{1,0:T(8,128)(2,1)S(1)} %get-tuple-element.10), channel_id=1, source_target_pairs={{0,2},{2,0},{4,6},{6,4},{8,10},{10,8},{12,14},{14,12},{16,18},{18,... | collective-permute-start | bytes 3145736 | tf_op jit(solution)/shard_map/ppermute | solution.py:48
  94.1 9.9 %collective-permute-start.9 = (bf16[1024,128]{1,0:T(8,128)(2,1)S(1)}, bf16[1024,128]{1,0:T(8,128)(2,1)S(1)}, u32[]{:S(2)}, u32[]{:S(2)}) collective-permute-start(bf16[1024,128]{1,0:T(8,128)(2,1)S(1)} %get-tuple-element.16), channel_id=1, source_target_pairs={{0,13},{1,12},{2,6},{3,7},{4,0},{5,1},{6,10},{7,11},{8,4},{9,5},{1... | collective-permute-start | bytes 786440 | tf_op jit(solution)/shard_map/ppermute | solution.py:44
  98.0 9.8 %collective-permute-start.8 = (bf16[1024,128]{1,0:T(8,128)(2,1)S(1)}, bf16[1024,128]{1,0:T(8,128)(2,1)S(1)}, u32[]{:S(2)}, u32[]{:S(2)}) collective-permute-start(bf16[1024,128]{1,0:T(8,128)(2,1)S(1)} %get-tuple-element.15), channel_id=1, source_target_pairs={{0,4},{1,5},{2,15},{3,14},{4,8},{5,9},{6,2},{7,3},{8,12},{9,13},{1... | collective-permute-start | bytes 786440 | tf_op jit(solution)/shard_map/ppermute | solution.py:44
  104.1 7.7 %collective-permute-start.10 = (bf16[1024,128]{1,0:T(8,128)(2,1)S(1)}, bf16[1024,128]{1,0:T(8,128)(2,1)S(1)}, u32[]{:S(2)}, u32[]{:S(2)}) collective-permute-start(bf16[1024,128]{1,0:T(8,128)(2,1)S(1)} %add_convert_fusion.1), channel_id=1, source_target_pairs={{0,13},{1,12},{2,6},{3,7},{4,0},{5,1},{6,10},{7,11},{8,4},{9,5},{1... | collective-permute-start | bytes 786440 | tf_op jit(solution)/shard_map/ppermute | solution.py:44
  111.9 23.6 %copy-start.8 = (f32[13,64]{1,0:T(8,128)S(1)}, f32[13,64]{1,0:T(8,128)}, u32[]{:S(2)}) copy-start(f32[13,64]{1,0:T(8,128)} %param.19) | copy-start | bytes 9988
  111.9 24.2 %copy-start.6 = (bf16[13,64,128]{2,1,0:T(8,128)(2,1)S(1)}, bf16[13,64,128]{2,1,0:T(8,128)(2,1)}, u32[]{:S(2)}) copy-start(bf16[13,64,128]{2,1,0:T(8,128)(2,1)} %param.18) | copy-start | bytes 638980

commit v5 on v4

--- a/solution.py
+++ b/solution.py
@@ -23,6 +23,8 @@
 PIECE = GROUPS * ROWS_DEV
 HALF = Z_LO * PIECE
 ROWS = CORES * HALF
+BITS = 14
+WORDS = POOL // 2
 
 across = [[g * COLUMN + k for g in range(GROUPS)] for k in range(COLUMN)]
 across_reps = [[d * REPS + r for d in group for r in range(REPS)] for group in across]
@@ -86,11 +88,14 @@
 
         def place(g, _):
             def some(i, _):
-                base = g * (POOL * samples) + i * unroll
+                base = g * (WORDS * samples) + i * unroll
                 bag = g * samples + i * unroll
                 for u in range(unroll):
+                    words = [ids_ref[base + (j * samples + u)] for j in range(WORDS)]
                     r = [
-                        tab[pl.ds(ids_ref[base + (j * samples + u)], 1), :] for j in range(POOL)
+                        tab[pl.ds(row, 1), :]
+                        for w in words
+                        for row in (w & (2**BITS - 1), w >> BITS)
                     ]
                     acc[pl.ds(bag + u, 1), :] = (r[0] + r[1]) + (r[2] + r[3])
                 return 0
@@ -108,7 +113,7 @@
         scratch_shapes=[
             pltpu.VMEM((ROWS + 8, EMB), f32),
             pltpu.VMEM((places * samples, EMB), f32),
-            pltpu.SMEM((places * POOL * samples,), i32),
+            pltpu.SMEM((places * WORDS * samples,), i32),
             pltpu.SemaphoreType.DMA,
         ],
         compiler_params=pltpu.CompilerParams(vmem_limit_bytes=10 << 20),
@@ -284,12 +289,14 @@
     got = exchange(payload)
     own = got[:, :ROWS_DEV].reshape(PIECE, EMB)
     high, low = got[:, ROWS_DEV : ROWS_DEV + pool], got[:, ROWS_DEV + pool :]
-    at = (high.astype(f32) * 128.0 + low.astype(f32)).astype(i32).reshape(-1)
+    at = (high.astype(f32) * 128.0 + low.astype(f32)).astype(i32)
+    words = (at[:, :WORDS] | at[:, WORDS:] << BITS).reshape(-1)
+    at = at.reshape(-1)
 
     one, three = send_z(own, -1), send_z(own, 1)
     two = send_z(one, -1)
     pieces = [own, one, two, three] + [swap(x) for x in (own, three, two, one)]
-    pooled = exchange(lookup(at, pieces, samples).reshape(GROUPS, samples, EMB))
+    pooled = exchange(lookup(words, pieces, samples).reshape(GROUPS, samples, EMB))
 
     crossed, pooled_grad = cross(
         bottom(dense_feats, bottom_w1, bottom_w2, bottom_w3),

time: 137 us -> 137 us (level)
  no operation moved by 1% of the time
where the time goes in v5:
time: 137 us
  blocking collectives  52.1 us (38%)
  waiting for transfers between devices  32 us (23%)
  Pallas kernels  23.3 us (17%)
  starting transfers between devices  22.7 us (17%)
  other arithmetic  3.95 us (3%)
  local copies, waits for them, and re-layouts  1.84 us (1%)
    all_to_all x2, blocking collectives, exchange(): lax.all_to_all(x, 'shard', split_axis=0, concat_axis=0, axis_index_groups...  28.9 us
    all_to_all x1, blocking collectives, exchange_reps(): lax.all_to_all(x, ('shard', 'rep'), split_axis=0, concat_axis=0, axis_ind...  23.2 us
    ppermute x6, waiting for transfers between devices, send_z(): return lax.ppermute(x, ('shard', 'rep'), along_z(step))  17.7 us
    ppermute x6, starting transfers between devices, send_z(): return lax.ppermute(x, ('shard', 'rep'), along_z(step))  17.3 us
    pallas_call x1, Pallas kernels, scatter(): pl.pallas_call(body, out_shape=[jax.ShapeDtypeStruct((HALF, EMB), f32), j...  11.9 us
    all_to_all x1, waiting for transfers between devices, exchange(): lax.all_to_all(x, 'shard', split_axis=0, concat_axis=0, axis_index_groups...  10.2 us
    pallas_call x1, Pallas kernels, lookup(): pl.pallas_call(body, out_shape=jax.ShapeDtypeStruct((places * samples, EM...  8.24 us
    all_to_all x1, starting transfers between devices, exchange(): lax.all_to_all(x, 'shard', split_axis=0, concat_axis=0, axis_index_groups...  4.76 us
  transfers between devices with their start and end apart: 12, of which 8 were waited for; matrix products, arithmetic and copies ran while one was open for 0% of the time, Pallas kernels for 0%

profile of v5, /device:TPU:2, one launch (start us, length us, event | category | flops | bytes accessed | tf_op | source)
XLA Modules:
  0.0 136.8 jit_solution(9278320673993389745)
XLA Ops:
  0.7 0.8 broadcast_shift-right-arithmetic_fusion
  1.5 1.0 fusion.2
  2.5 14.9 %all_to_all.20 = bf16[16,72,128]{2,1,0:T(8,128)(2,1)S(1)} all-to-all(bf16[16,72,128]{2,1,0:T(8,128)(2,1)S(1)} %fusion.2), channel_id=1, replica_groups={{0,16,32,48,64,80,96,112,128,144,160,176,192,208,224,240},{2,18,34,50,6..., dimensions={0} | all-to-all | bytes 589824 | tf_op jit(solution)/shard_map/all_to_all | solution.py:54
  17.5 5.9 %collective-permute-start = (bf16[1024,128]{1,0:T(8,128)(2,1)S(1)}, bf16[1024,128]{1,0:T(8,128)(2,1)S(1)}, u32[]{:S(2)}, u32[]{:S(2)}) collective-permute-start(bf16[1024,128]{1,0:T(8,128)(2,1)S(1)} %bitcast.14), channel_id=1, source_target_pairs={{0,13},{1,12},{2,6},{3,7},{4,0},{5,1},{6,10},{7,11},{8,4},{9,5},{1... | collective-permute-start | bytes 786440 | tf_op jit(solution)/shard_map/ppermute | solution.py:46
  23.4 4.5 %collective-permute-done.refs_1_ = bf16[1024,128]{1,0:T(8,128)(2,1)S(1)} collective-permute-done((bf16[1024,128]{1,0:T(8,128)(2,1)S(1)}, bf16[1024,128]{1,0:T(8,128)(2,1)S(1)}, u32[]{:S(2)}, u32[]{:S(2)}) %collective-permute-start) | collective-permute-done | bytes 262176 | tf_op jit(solution)/shard_map/ppermute | solution.py:46
  27.9 3.7 %collective-permute-start.1 = (bf16[1024,128]{1,0:T(8,128)(2,1)S(1)}, bf16[1024,128]{1,0:T(8,128)(2,1)S(1)}, u32[]{:S(2)}, u32[]{:S(2)}) collective-permute-start(bf16[1024,128]{1,0:T(8,128)(2,1)S(1)} %collective-permute-done.refs_1_), channel_id=1, source_target_pairs={{0,13},{1,12},{2,6},{3,7},{4,0},{5,1},{6,10},{7,11},{8,4},{9,5},{1... | collective-permute-start | bytes 786440 | tf_op jit(solution)/shard_map/ppermute | solution.py:46
  31.6 0.5 collective-permute-start.6
  32.5 3.0 %collective-permute-done.1.refs_2_ = bf16[1024,128]{1,0:T(8,128)(2,1)S(1)} collective-permute-done((bf16[1024,128]{1,0:T(8,128)(2,1)S(1)}, bf16[1024,128]{1,0:T(8,128)(2,1)S(1)}, u32[]{:S(2)}, u32[]{:S(2)}) %collective-permute-start.1) | collective-permute-done | bytes 262176 | tf_op jit(solution)/shard_map/ppermute | solution.py:46
  35.6 1.4 %collective-permute-done.5.refs_6_ = bf16[1024,128]{1,0:T(8,128)(2,1)S(1)} collective-permute-done((bf16[1024,128]{1,0:T(8,128)(2,1)S(1)}, bf16[1024,128]{1,0:T(8,128)(2,1)S(1)}, u32[]{:S(2)}, u32[]{:S(2)}) %collective-permute-start.5) | collective-permute-done | bytes 262176 | tf_op jit(solution)/shard_map/ppermute | solution.py:50
  37.0 8.2 %lookup.1 = bf16[2048,128]{1,0:T(8,128)(2,1)} custom-call(s32[4096]{0:T(1024)S(1)} %bitcast.19, bf16[1024,128]{1,0:T(8,128)(2,1)S(1)} %bitcast.17, bf16[1024,128]{1,0:T(8,128)(2,1)S(1)} %collective-permute-done.refs_1_, bf16[1024,128]{1,0:T(8,128)(2,1)S(1)} %collective-permute-done.1.refs_2_, bf16[1024,128]{1,0:T(8,128)(2,1)S(1)} %collective-permute-done.2.refs_3_, ...), custom_call_target="tpu_custom_call" | custom-call | tf_op jit(solution)/shard_map/lookup/pallas_call | solution.py:108
  45.3 4.8 %all-to-all-start.1 = ((bf16[16,128,128]{2,1,0:T(8,128)(2,1)}), bf16[16,128,128]{2,1,0:T(8,128)(2,1)S(1)}, u32[]{:S(2)}, u32[]{:S(2)}) async-start(bf16[16,128,128]{2,1,0:T(8,128)(2,1)} %bitcast.4), calls=%async_computation.1 | async-start | bytes 1048576 | tf_op jit(solution)/shard_map/all_to_all | solution.py:54
  50.7 10.2 %all-to-all-done.1.pooled_ref = bf16[16,128,128]{2,1,0:T(8,128)(2,1)S(1)} async-done(((bf16[16,128,128]{2,1,0:T(8,128)(2,1)}), bf16[16,128,128]{2,1,0:T(8,128)(2,1)S(1)}, u32[]{:S(2)}, u32[]{:S(2)}) %all-to-all-start.1) | async-done | bytes 524320 | tf_op jit(solution)/shard_map/all_to_all | solution.py:54
  60.9 1.5 %copy-done.1 = bf16[512,1792]{1,0:T(8,128)(2,1)S(1)} copy-done((bf16[512,1792]{1,0:T(8,128)(2,1)S(1)}, bf16[512,1792]{1,0:T(8,128)(2,1)}, u32[]{:S(2)}) %copy-start.1) | copy-done | bytes 1835032
  62.4 2.7 %cross.1 = (bf16[128,1792]{1,0:T(8,128)(2,1)}, bf16[16,128,128]{2,1,0:T(8,128)(2,1)S(1)}) custom-call(bf16[128,128]{1,0:T(8,128)(2,1)S(1)} %bottom.1.third_ref, bf16[16,128,128]{2,1,0:T(8,128)(2,1)S(1)} %all-to-all-done.1.pooled_ref, bf16[1792,512]{1,0:T(8,128)(2,1)S(1)} %copy-done, bf16[512,1792]{1,0:T(8,128)(2,1)S(1)} %copy-done.1, ...), custom_call_target="tpu_custom_call" | custom-call | tf_op jit(solution)/shard_map/cross/pallas_call | solution.py:247
  65.1 14.0 %all_to_all.21 = bf16[16,128,128]{2,1,0:T(8,128)(2,1)S(1)} all-to-all(bf16[16,128,128]{2,1,0:T(8,128)(2,1)S(1)} %get-tuple-element.8), channel_id=1, replica_groups={{0,16,32,48,64,80,96,112,128,144,160,176,192,208,224,240},{2,18,34,50,6..., dimensions={0} | all-to-all | bytes 1048576 | tf_op jit(solution)/shard_map/all_to_all | solution.py:54
  79.1 11.9 %scatter.1 = (f32[4096,128]{1,0:T(8,128)S(1)}, bf16[4096,128]{1,0:T(8,128)(2,1)S(1)}) custom-call(s32[8192]{0:T(1024)S(1)} %bitcast.18, bf16[2048,128]{1,0:T(8,128)(2,1)S(1)} %bitcast.13), custom_call_target="tpu_custom_call" | custom-call | tf_op jit(solution)/shard_map/scatter/pallas_call | solution.py:175
  91.1 2.6 %collective-permute-done.7 = bf16[4096,128]{1,0:T(8,128)(2,1)S(1)} collective-permute-done((bf16[4096,128]{1,0:T(8,128)(2,1)S(1)}, bf16[4096,128]{1,0:T(8,128)(2,1)S(1)}, u32[]{:S(2)}, u32[]{:S(2)}) %collective-permute-start.7) | collective-permute-done | bytes 1048608 | tf_op jit(solution)/shard_map/ppermute | solution.py:50
  93.8 3.9 %collective-permute-start.9 = (bf16[1024,128]{1,0:T(8,128)(2,1)S(1)}, bf16[1024,128]{1,0:T(8,128)(2,1)S(1)}, u32[]{:S(2)}, u32[]{:S(2)}) collective-permute-start(bf16[1024,128]{1,0:T(8,128)(2,1)S(1)} %get-tuple-element.16), channel_id=1, source_target_pairs={{0,13},{1,12},{2,6},{3,7},{4,0},{5,1},{6,10},{7,11},{8,4},{9,5},{1... | collective-permute-start | bytes 786440 | tf_op jit(solution)/shard_map/ppermute | solution.py:46
  97.8 6.0 %collective-permute-done.9 = bf16[1024,128]{1,0:T(8,128)(2,1)S(1)} collective-permute-done((bf16[1024,128]{1,0:T(8,128)(2,1)S(1)}, bf16[1024,128]{1,0:T(8,128)(2,1)S(1)}, u32[]{:S(2)}, u32[]{:S(2)}) %collective-permute-start.9) | collective-permute-done | bytes 262176 | tf_op jit(solution)/shard_map/ppermute | solution.py:46
  103.8 3.8 %collective-permute-start.10 = (bf16[1024,128]{1,0:T(8,128)(2,1)S(1)}, bf16[1024,128]{1,0:T(8,128)(2,1)S(1)}, u32[]{:S(2)}, u32[]{:S(2)}) collective-permute-start(bf16[1024,128]{1,0:T(8,128)(2,1)S(1)} %add_convert_fusion.1), channel_id=1, source_target_pairs={{0,13},{1,12},{2,6},{3,7},{4,0},{5,1},{6,10},{7,11},{8,4},{9,5},{1... | collective-permute-start | bytes 786440 | tf_op jit(solution)/shard_map/ppermute | solution.py:46
  107.6 3.9 %collective-permute-done.10 = bf16[1024,128]{1,0:T(8,128)(2,1)S(1)} collective-permute-done((bf16[1024,128]{1,0:T(8,128)(2,1)S(1)}, bf16[1024,128]{1,0:T(8,128)(2,1)S(1)}, u32[]{:S(2)}, u32[]{:S(2)}) %collective-permute-start.10) | collective-permute-done | bytes 262176 | tf_op jit(solution)/shard_map/ppermute | solution.py:46
  111.8 23.2 %all_to_all.22 = bf16[32,64,128]{2,1,0:T(8,128)(2,1)S(1)} all-to-all(bf16[32,64,128]{2,1,0:T(8,128)(2,1)S(1)} %bitcast.20), channel_id=1, replica_groups={{0,1,16,17,32,33,48,49,64,65,80,81,96,97,112,113,128,129,144,145,160,16..., dimensions={0} | all-to-all | bytes 1048576 | tf_op jit(solution)/shard_map/all_to_all | solution.py:60
  135.2 0.6 sqrt_add_fusion
  135.8 0.9 divide_subtract_fusion
  (45 shorter events, 2.0 us)
Async XLA Ops:
  17.4 32.6 %copy-start.7 = (f32[1792]{0:T(1024)S(1)}, f32[1792]{0:T(1024)}, u32[]{:S(2)}) copy-start(f32[1792]{0:T(1024)} %param.22) | copy-start | bytes 21508
  17.4 32.7 %copy-start.9 = (bf16[128,13]{0,1:T(8,128)(2,1)S(1)}, bf16[128,13]{0,1:T(8,128)(2,1)}, u32[]{:S(2)}) copy-start(bf16[128,13]{0,1:T(8,128)(2,1)} %param.12) | copy-start | bytes 9988
  17.4 32.8 %copy-start.3 = (bf16[512,256]{1,0:T(8,128)(2,1)S(1)}, bf16[512,256]{1,0:T(8,128)(2,1)}, u32[]{:S(2)}) copy-start(bf16[512,256]{1,0:T(8,128)(2,1)} %w2_ref.1) | copy-start | bytes 786436
  17.4 32.8 %copy-start.4 = (bf16[256,128]{1,0:T(8,128)(2,1)S(1)}, bf16[256,128]{1,0:T(8,128)(2,1)}, u32[]{:S(2)}) copy-start(bf16[256,128]{1,0:T(8,128)(2,1)} %w3_ref.1) | copy-start | bytes 196612
  17.4 32.8 %copy-start.5 = (bf16[13,512]{1,0:T(8,128)(2,1)S(1)}, bf16[13,512]{1,0:T(8,128)(2,1)}, u32[]{:S(2)}) copy-start(bf16[13,512]{1,0:T(8,128)(2,1)} %w1_ref.1) | copy-start | bytes 39940
  17.5 10.5 %collective-permute-start = (bf16[1024,128]{1,0:T(8,128)(2,1)S(1)}, bf16[1024,128]{1,0:T(8,128)(2,1)S(1)}, u32[]{:S(2)}, u32[]{:S(2)}) collective-permute-start(bf16[1024,128]{1,0:T(8,128)(2,1)S(1)} %bitcast.14), channel_id=1, source_target_pairs={{0,13},{1,12},{2,6},{3,7},{4,0},{5,1},{6,10},{7,11},{8,4},{9,5},{1... | collective-permute-start | bytes 786440 | tf_op jit(solution)/shard_map/ppermute | solution.py:46
  23.4 9.1 %collective-permute-start.2 = (bf16[1024,128]{1,0:T(8,128)(2,1)S(1)}, bf16[1024,128]{1,0:T(8,128)(2,1)S(1)}, u32[]{:S(2)}, u32[]{:S(2)}) collective-permute-start(bf16[1024,128]{1,0:T(8,128)(2,1)S(1)} %bitcast.15), channel_id=1, source_target_pairs={{0,4},{1,5},{2,15},{3,14},{4,8},{5,9},{6,2},{7,3},{8,12},{9,13},{1... | collective-permute-start | bytes 786440 | tf_op jit(solution)/shard_map/ppermute | solution.py:46
  27.9 7.6 %collective-permute-start.1 = (bf16[1024,128]{1,0:T(8,128)(2,1)S(1)}, bf16[1024,128]{1,0:T(8,128)(2,1)S(1)}, u32[]{:S(2)}, u32[]{:S(2)}) collective-permute-start(bf16[1024,128]{1,0:T(8,128)(2,1)S(1)} %collective-permute-done.refs_1_), channel_id=1, source_target_pairs={{0,13},{1,12},{2,6},{3,7},{4,0},{5,1},{6,10},{7,11},{8,4},{9,5},{1... | collective-permute-start | bytes 786440 | tf_op jit(solution)/shard_map/ppermute | solution.py:46
  31.6 4.0 %collective-permute-start.3 = (bf16[1024,128]{1,0:T(8,128)(2,1)S(1)}, bf16[1024,128]{1,0:T(8,128)(2,1)S(1)}, u32[]{:S(2)}, u32[]{:S(2)}) collective-permute-start(bf16[1024,128]{1,0:T(8,128)(2,1)S(1)} %bitcast.16), channel_id=1, source_target_pairs={{0,2},{2,0},{4,6},{6,4},{8,10},{10,8},{12,14},{14,12},{16,18},{18,... | collective-permute-start | bytes 786440 | tf_op jit(solution)/shard_map/ppermute | solution.py:50
  31.6 4.0 %collective-permute-start.6 = (bf16[1024,128]{1,0:T(8,128)(2,1)S(1)}, bf16[1024,128]{1,0:T(8,128)(2,1)S(1)}, u32[]{:S(2)}, u32[]{:S(2)}) collective-permute-start(bf16[1024,128]{1,0:T(8,128)(2,1)S(1)} %collective-permute-done.refs_1_), channel_id=1, source_target_pairs={{0,2},{2,0},{4,6},{6,4},{8,10},{10,8},{12,14},{14,12},{16,18},{18,... | collective-permute-start | bytes 786440 | tf_op jit(solution)/shard_map/ppermute | solution.py:50
  32.5 3.1 %collective-permute-start.4 = (bf16[1024,128]{1,0:T(8,128)(2,1)S(1)}, bf16[1024,128]{1,0:T(8,128)(2,1)S(1)}, u32[]{:S(2)}, u32[]{:S(2)}) collective-permute-start(bf16[1024,128]{1,0:T(8,128)(2,1)S(1)} %collective-permute-done.2.refs_3_), channel_id=1, source_target_pairs={{0,2},{2,0},{4,6},{6,4},{8,10},{10,8},{12,14},{14,12},{16,18},{18,... | collective-permute-start | bytes 786440 | tf_op jit(solution)/shard_map/ppermute | solution.py:50
  35.5 1.5 %collective-permute-start.5 = (bf16[1024,128]{1,0:T(8,128)(2,1)S(1)}, bf16[1024,128]{1,0:T(8,128)(2,1)S(1)}, u32[]{:S(2)}, u32[]{:S(2)}) collective-permute-start(bf16[1024,128]{1,0:T(8,128)(2,1)S(1)} %collective-permute-done.1.refs_2_), channel_id=1, source_target_pairs={{0,2},{2,0},{4,6},{6,4},{8,10},{10,8},{12,14},{14,12},{16,18},{18,... | collective-permute-start | bytes 786440 | tf_op jit(solution)/shard_map/ppermute | solution.py:50
  35.5 25.4 %copy-start = (bf16[1792,512]{1,0:T(8,128)(2,1)S(1)}, bf16[1792,512]{1,0:T(8,128)(2,1)}, u32[]{:S(2)}) copy-start(bf16[1792,512]{1,0:T(8,128)(2,1)} %down_ref.1) | copy-start | bytes 5505028
  35.5 25.4 %copy-start.2 = (bf16[128,1792]{1,0:T(8,128)(2,1)S(1)}, bf16[128,1792]{1,0:T(8,128)(2,1)}, u32[]{:S(2)}) copy-start(bf16[128,1792]{1,0:T(8,128)(2,1)} %cot_ref.1) | copy-start | bytes 1376260
  45.3 15.6 %all-to-all-start.1 = ((bf16[16,128,128]{2,1,0:T(8,128)(2,1)}), bf16[16,128,128]{2,1,0:T(8,128)(2,1)S(1)}, u32[]{:S(2)}, u32[]{:S(2)}) async-start(bf16[16,128,128]{2,1,0:T(8,128)(2,1)} %bitcast.4), calls=%async_computation.1 | async-start | bytes 1048576 | tf_op jit(solution)/shard_map/all_to_all | solution.py:54
  60.9 1.5 %copy-start.1 = (bf16[512,1792]{1,0:T(8,128)(2,1)S(1)}, bf16[512,1792]{1,0:T(8,128)(2,1)}, u32[]{:S(2)}) copy-start(bf16[512,1792]{1,0:T(8,128)(2,1)} %up_ref.1) | copy-start | bytes 5505028
  91.0 2.7 %collective-permute-start.7 = (bf16[4096,128]{1,0:T(8,128)(2,1)S(1)}, bf16[4096,128]{1,0:T(8,128)(2,1)S(1)}, u32[]{:S(2)}, u32[]{:S(2)}) collective-permute-start(bf16[4096,128]{1,0:T(8,128)(2,1)S(1)} %get-tuple-element.10), channel_id=1, source_target_pairs={{0,2},{2,0},{4,6},{6,4},{8,10},{10,8},{12,14},{14,12},{16,18},{18,... | collective-permute-start | bytes 3145736 | tf_op jit(solution)/shard_map/ppermute | solution.py:50
  93.8 9.9 %collective-permute-start.9 = (bf16[1024,128]{1,0:T(8,128)(2,1)S(1)}, bf16[1024,128]{1,0:T(8,128)(2,1)S(1)}, u32[]{:S(2)}, u32[]{:S(2)}) collective-permute-start(bf16[1024,128]{1,0:T(8,128)(2,1)S(1)} %get-tuple-element.16), channel_id=1, source_target_pairs={{0,13},{1,12},{2,6},{3,7},{4,0},{5,1},{6,10},{7,11},{8,4},{9,5},{1... | collective-permute-start | bytes 786440 | tf_op jit(solution)/shard_map/ppermute | solution.py:46
  97.8 9.8 %collective-permute-start.8 = (bf16[1024,128]{1,0:T(8,128)(2,1)S(1)}, bf16[1024,128]{1,0:T(8,128)(2,1)S(1)}, u32[]{:S(2)}, u32[]{:S(2)}) collective-permute-start(bf16[1024,128]{1,0:T(8,128)(2,1)S(1)} %get-tuple-element.15), channel_id=1, source_target_pairs={{0,4},{1,5},{2,15},{3,14},{4,8},{5,9},{6,2},{7,3},{8,12},{9,13},{1... | collective-permute-start | bytes 786440 | tf_op jit(solution)/shard_map/ppermute | solution.py:46
  103.8 7.7 %collective-permute-start.10 = (bf16[1024,128]{1,0:T(8,128)(2,1)S(1)}, bf16[1024,128]{1,0:T(8,128)(2,1)S(1)}, u32[]{:S(2)}, u32[]{:S(2)}) collective-permute-start(bf16[1024,128]{1,0:T(8,128)(2,1)S(1)} %add_convert_fusion.1), channel_id=1, source_target_pairs={{0,13},{1,12},{2,6},{3,7},{4,0},{5,1},{6,10},{7,11},{8,4},{9,5},{1... | collective-permute-start | bytes 786440 | tf_op jit(solution)/shard_map/ppermute | solution.py:46
  111.6 23.6 %copy-start.8 = (f32[13,64]{1,0:T(8,128)S(1)}, f32[13,64]{1,0:T(8,128)}, u32[]{:S(2)}) copy-start(f32[13,64]{1,0:T(8,128)} %param.19) | copy-start | bytes 9988
  111.6 24.2 %copy-start.6 = (bf16[13,64,128]{2,1,0:T(8,128)(2,1)S(1)}, bf16[13,64,128]{2,1,0:T(8,128)(2,1)}, u32[]{:S(2)}) copy-start(bf16[13,64,128]{2,1,0:T(8,128)(2,1)} %param.18) | copy-start | bytes 638980
